TPU v7x, 32 devices: a whole 2x2x4 slice. The times are simulated.
32 devices in a mesh: rep: 4 (over y, x), shard: 4 (over z), seq: 2 (over core).
Axes of the slice: x: 2, y: 2, z: 4, core: 2. Of those that a mesh axis runs over, the one named last changes fastest.
Arguments:
- tokens: bfloat16 [16, 256, 1024], P(('rep', 'shard'), 'seq'), may hold values from -40 to 40
- key_valid: int32 [16, 256], P(('rep', 'shard')), may hold values from 0 to 1, as said below
- cotangent: bfloat16 [16, 256, 1024], P(('rep', 'shard'), 'seq'), may hold values from -6 to 6
- attngain: bfloat16 [1024], P(('shard', 'seq')), may hold values from 0.5 to 1.5
- attnshift: bfloat16 [1024], P(('shard', 'seq')), may hold values from -4 to 4
- qkvweight: bfloat16 [1024, 3072], P(('shard', 'seq')), may hold values from -3 to 3
- querybias: bfloat16 [1024], P(('shard', 'seq')), may hold values from -4 to 4
- valuebias: bfloat16 [1024], P(('shard', 'seq')), may hold values from -4 to 4
- projweight: bfloat16 [1024, 1024], P(('shard', 'seq')), may hold values from -4 to 4
- projbias: bfloat16 [1024], P(('shard', 'seq')), may hold values from -4 to 4
- attnscale: bfloat16 [1024], P(('shard', 'seq')), may hold values from 0.5 to 1.5
- mlpgain: bfloat16 [1024], P(('shard', 'seq')), may hold values from 0.5 to 1.5
- mlpshift: bfloat16 [1024], P(('shard', 'seq')), may hold values from -4 to 4
- upweight: bfloat16 [1024, 4096], P(('shard', 'seq')), may hold values from -0.1875 to 0.1875
- upbias: bfloat16 [4096], P(('shard', 'seq')), may hold values from -4 to 4
- downweight: bfloat16 [4096, 1024], P(('shard', 'seq')), may hold values from -0.09375 to 0.09375
- downbias: bfloat16 [1024], P(('shard', 'seq')), may hold values from -4 to 4
- mlpscale: bfloat16 [1024], P(('shard', 'seq')), may hold values from 0.5 to 1.5
Outputs:
- block_out: float32 [16, 256, 1024], P(('rep', 'shard'), 'seq')
- grad_tokens: float32 [16, 256, 1024], P(('rep', 'shard'), 'seq')
- grad_attngain: float32 [1024], P(('shard', 'seq'))
- grad_attnshift: float32 [1024], P(('shard', 'seq'))
- grad_qkvweight: float32 [1024, 3072], P(('shard', 'seq'))
- grad_querybias: float32 [1024], P(('shard', 'seq'))
- grad_valuebias: float32 [1024], P(('shard', 'seq'))
- grad_projweight: float32 [1024, 1024], P(('shard', 'seq'))
- grad_projbias: float32 [1024], P(('shard', 'seq'))
- grad_attnscale: float32 [1024], P(('shard', 'seq'))
- grad_mlpgain: float32 [1024], P(('shard', 'seq'))
- grad_mlpshift: float32 [1024], P(('shard', 'seq'))
- grad_upweight: float32 [1024, 4096], P(('shard', 'seq'))
- grad_upbias: float32 [4096], P(('shard', 'seq'))
- grad_downweight: float32 [4096, 1024], P(('shard', 'seq'))
- grad_downbias: float32 [1024], P(('shard', 'seq'))
- grad_mlpscale: float32 [1024], P(('shard', 'seq'))
Inputs may be any that keep to these rules, and one draw needn't show every extreme that they name: `key_valid`: in each image the valid positions are its first ones, from 128 to 256 of them; some image has exactly 128, another all 256.
All inputs are finite; a program needn't handle non-finite values.
Results may differ from a plain program's by a relative error of at most 0.011.
Values may be sent and summed in bfloat16 or wider, within the bound.
A program may use at most 192 MiB of HBM per device.

v0:
```python
import jax
import jax.numpy as jnp
from jax import lax
from jax.sharding import PartitionSpec as P

HEADS = 16
HEAD = 64


EPSILON = 1e-06
SCORE_SCALE = 0.125
ROOT_HALF = 0.7071067811865476
INV_ROOT_TAU = 0.3989422804014327
MASKED = -1e30


def norm_forward(hidden):
    center = hidden - jnp.mean(hidden, axis=-1, keepdims=True)
    spread = lax.rsqrt(jnp.mean(center * center, axis=-1, keepdims=True) + EPSILON)
    return (center * spread, spread)


def norm_backward(grad_norm, normed, spread):
    first_mean = jnp.mean(grad_norm, axis=-1, keepdims=True)
    second_mean = jnp.mean(grad_norm * normed, axis=-1, keepdims=True)
    return spread * (grad_norm - first_mean - normed * second_mean)


def gelu_pair(hidden):
    cumulative = 0.5 * (1.0 + lax.erf(hidden * ROOT_HALF))
    gelu_slope = cumulative + hidden * jnp.exp(-0.5 * hidden * hidden) * INV_ROOT_TAU
    return (hidden * cumulative, gelu_slope)


def split_heads(matrix, images):
    return matrix.reshape(images, -1, HEADS, HEAD)


def score_block(query_heads, key_heads, key_valid):
    scores = (
        jnp.einsum("iqhe,ikhe->ihqk", query_heads, key_heads, preferred_element_type=jnp.float32)
        * SCORE_SCALE
    )
    return jnp.where((key_valid > 0)[:, None, None, :], scores, MASKED)


def contract_rows(left, right):
    return lax.dot_general(
        left, right, (((0,), (0,)), ((), ())), preferred_element_type=jnp.float32
    )


def times_transposed(left, weight):
    return lax.dot_general(
        left, weight, (((1,), (1,)), ((), ())), preferred_element_type=jnp.float32
    )


def per_device(
    tokens,
    key_valid,
    cotangent,
    attngain,
    attnshift,
    qkvweight,
    querybias,
    valuebias,
    projweight,
    projbias,
    attnscale,
    mlpgain,
    mlpshift,
    upweight,
    upbias,
    downweight,
    downbias,
    mlpscale,
):
    images, tok_rows, feat_width = tokens.shape
    total_rows = images * tok_rows
    gain_one, shift_one, qkv_full, qbias_full, vbias_full, proj_full, pbias_full, scale_one = (
        lax.all_gather(attngain, ("shard", "seq"), axis=0, tiled=True),
        lax.all_gather(attnshift, ("shard", "seq"), axis=0, tiled=True),
        lax.all_gather(qkvweight, ("shard", "seq"), axis=0, tiled=True),
        lax.all_gather(querybias, ("shard", "seq"), axis=0, tiled=True),
        lax.all_gather(valuebias, ("shard", "seq"), axis=0, tiled=True),
        lax.all_gather(projweight, ("shard", "seq"), axis=0, tiled=True),
        lax.all_gather(projbias, ("shard", "seq"), axis=0, tiled=True),
        lax.all_gather(attnscale, ("shard", "seq"), axis=0, tiled=True),
    )
    hidden = tokens.reshape(total_rows, feat_width).astype(jnp.float32)
    normed_one, spread_one = norm_forward(hidden)
    act_one = (normed_one * gain_one.astype(jnp.float32) + shift_one.astype(jnp.float32)).astype(
        jnp.bfloat16
    )
    mixed = jnp.dot(act_one, qkv_full, preferred_element_type=jnp.float32)
    queries = (mixed[:, :feat_width] + qbias_full.astype(jnp.float32)).astype(jnp.bfloat16)
    key_local = (
        mixed[:, feat_width : 2 * feat_width]
        .astype(jnp.bfloat16)
        .reshape(images, tok_rows, feat_width)
    )
    value_local = (
        (mixed[:, 2 * feat_width :] + vbias_full.astype(jnp.float32))
        .astype(jnp.bfloat16)
        .reshape(images, tok_rows, feat_width)
    )
    key_all, value_all = (
        lax.all_gather(key_local, "seq", axis=1, tiled=True),
        lax.all_gather(value_local, "seq", axis=1, tiled=True),
    )
    query_heads = split_heads(queries, images)
    key_heads = split_heads(key_all, images)
    value_heads = split_heads(value_all, images)
    scores = score_block(query_heads, key_heads, key_valid)
    top_score = jnp.max(scores, axis=-1, keepdims=True)
    log_total = top_score + jnp.log(jnp.sum(jnp.exp(scores - top_score), axis=-1, keepdims=True))
    prob_low = jnp.exp(scores - log_total).astype(jnp.bfloat16)
    attended = (
        jnp.einsum("ihqk,ikhe->iqhe", prob_low, value_heads, preferred_element_type=jnp.float32)
        .reshape(total_rows, feat_width)
        .astype(jnp.bfloat16)
    )
    branch_one = jnp.dot(
        attended, proj_full, preferred_element_type=jnp.float32
    ) + pbias_full.astype(jnp.float32)
    middle = hidden + scale_one.astype(jnp.float32) * branch_one
    gain_two, shift_two, up_full, upb_full, down_full, downb_full, scale_two = (
        lax.all_gather(mlpgain, ("shard", "seq"), axis=0, tiled=True),
        lax.all_gather(mlpshift, ("shard", "seq"), axis=0, tiled=True),
        lax.all_gather(upweight, ("shard", "seq"), axis=0, tiled=True),
        lax.all_gather(upbias, ("shard", "seq"), axis=0, tiled=True),
        lax.all_gather(downweight, ("shard", "seq"), axis=0, tiled=True),
        lax.all_gather(downbias, ("shard", "seq"), axis=0, tiled=True),
        lax.all_gather(mlpscale, ("shard", "seq"), axis=0, tiled=True),
    )
    normed_two, spread_two = norm_forward(middle)
    act_two = (normed_two * gain_two.astype(jnp.float32) + shift_two.astype(jnp.float32)).astype(
        jnp.bfloat16
    )
    inner_pre = jnp.dot(act_two, up_full, preferred_element_type=jnp.float32) + upb_full.astype(
        jnp.float32
    )
    activated, gelu_slope = gelu_pair(inner_pre)
    act_three = activated.astype(jnp.bfloat16)
    branch_two = jnp.dot(
        act_three, down_full, preferred_element_type=jnp.float32
    ) + downb_full.astype(jnp.float32)
    block_out = middle + scale_two.astype(jnp.float32) * branch_two
    out_grad = cotangent.reshape(total_rows, feat_width).astype(jnp.float32)
    mlpscale_grad = jnp.sum(out_grad * branch_two, axis=0)
    branch_grad = out_grad * scale_two.astype(jnp.float32)
    downbias_grad = jnp.sum(branch_grad, axis=0)
    branch_low = branch_grad.astype(jnp.bfloat16)
    downweight_grad = contract_rows(act_three, branch_low)
    inner_grad = times_transposed(branch_low, down_full) * gelu_slope
    upbias_grad = jnp.sum(inner_grad, axis=0)
    inner_low = inner_grad.astype(jnp.bfloat16)
    upweight_grad = contract_rows(act_two, inner_low)
    acttwo_grad = times_transposed(inner_low, up_full)
    mlpgain_grad = jnp.sum(acttwo_grad * normed_two, axis=0)
    mlpshift_grad = jnp.sum(acttwo_grad, axis=0)
    middle_grad = out_grad + norm_backward(
        acttwo_grad * gain_two.astype(jnp.float32), normed_two, spread_two
    )
    mlp_part = (
        lax.psum_scatter(mlpgain_grad, ("shard", "seq"), scatter_dimension=0, tiled=True),
        lax.psum_scatter(mlpshift_grad, ("shard", "seq"), scatter_dimension=0, tiled=True),
        lax.psum_scatter(upweight_grad, ("shard", "seq"), scatter_dimension=0, tiled=True),
        lax.psum_scatter(upbias_grad, ("shard", "seq"), scatter_dimension=0, tiled=True),
        lax.psum_scatter(downweight_grad, ("shard", "seq"), scatter_dimension=0, tiled=True),
        lax.psum_scatter(downbias_grad, ("shard", "seq"), scatter_dimension=0, tiled=True),
        lax.psum_scatter(mlpscale_grad, ("shard", "seq"), scatter_dimension=0, tiled=True),
    )
    mlp_total = lax.psum(
        (mlp_part[0], mlp_part[1], mlp_part[2], mlp_part[3], mlp_part[4], mlp_part[5], mlp_part[6]),
        "rep",
    )
    attnscale_grad = jnp.sum(middle_grad * branch_one, axis=0)
    branchone_grad = middle_grad * scale_one.astype(jnp.float32)
    projbias_grad = jnp.sum(branchone_grad, axis=0)
    proj_low = branchone_grad.astype(jnp.bfloat16)
    projweight_grad = contract_rows(attended, proj_low)
    attn_back = times_transposed(proj_low, proj_full).astype(jnp.bfloat16)
    back_heads = split_heads(attn_back, images)
    scores = score_block(query_heads, key_heads, key_valid)
    probs = jnp.exp(scores - log_total)
    prob_low = probs.astype(jnp.bfloat16)
    prob_grad = jnp.einsum(
        "iqhe,ikhe->ihqk", back_heads, value_heads, preferred_element_type=jnp.float32
    )
    row_dot = jnp.sum(probs * prob_grad, axis=-1, keepdims=True)
    score_low = (probs * (prob_grad - row_dot)).astype(jnp.bfloat16)
    query_grad = (
        jnp.einsum("ihqk,ikhe->iqhe", score_low, key_heads, preferred_element_type=jnp.float32)
        * SCORE_SCALE
    ).reshape(total_rows, feat_width)
    key_part = (
        jnp.einsum("ihqk,iqhe->ikhe", score_low, query_heads, preferred_element_type=jnp.float32)
        * SCORE_SCALE
    ).reshape(images, -1, feat_width)
    value_part = jnp.einsum(
        "ihqk,iqhe->ikhe", prob_low, back_heads, preferred_element_type=jnp.float32
    ).reshape(images, -1, feat_width)
    key_grad, value_grad = (
        lax.psum_scatter(key_part, "seq", scatter_dimension=1, tiled=True),
        lax.psum_scatter(value_part, "seq", scatter_dimension=1, tiled=True),
    )
    key_grad = key_grad.reshape(total_rows, feat_width)
    value_grad = value_grad.reshape(total_rows, feat_width)
    querybias_grad = jnp.sum(query_grad, axis=0)
    valuebias_grad = jnp.sum(value_grad, axis=0)
    mixed_low = jnp.concatenate([query_grad, key_grad, value_grad], axis=1).astype(jnp.bfloat16)
    qkvweight_grad = contract_rows(act_one, mixed_low)
    actone_grad = times_transposed(mixed_low, qkv_full)
    attngain_grad = jnp.sum(actone_grad * normed_one, axis=0)
    attnshift_grad = jnp.sum(actone_grad, axis=0)
    tokens_grad = middle_grad + norm_backward(
        actone_grad * gain_one.astype(jnp.float32), normed_one, spread_one
    )
    attn_part = (
        lax.psum_scatter(attngain_grad, ("shard", "seq"), scatter_dimension=0, tiled=True),
        lax.psum_scatter(attnshift_grad, ("shard", "seq"), scatter_dimension=0, tiled=True),
        lax.psum_scatter(qkvweight_grad, ("shard", "seq"), scatter_dimension=0, tiled=True),
        lax.psum_scatter(querybias_grad, ("shard", "seq"), scatter_dimension=0, tiled=True),
        lax.psum_scatter(valuebias_grad, ("shard", "seq"), scatter_dimension=0, tiled=True),
        lax.psum_scatter(projweight_grad, ("shard", "seq"), scatter_dimension=0, tiled=True),
        lax.psum_scatter(projbias_grad, ("shard", "seq"), scatter_dimension=0, tiled=True),
        lax.psum_scatter(attnscale_grad, ("shard", "seq"), scatter_dimension=0, tiled=True),
    )
    attn_total = lax.psum(
        (
            attn_part[0],
            attn_part[1],
            attn_part[2],
            attn_part[3],
            attn_part[4],
            attn_part[5],
            attn_part[6],
            attn_part[7],
        ),
        "rep",
    )
    return (
        block_out.reshape(images, tok_rows, feat_width),
        tokens_grad.reshape(images, tok_rows, feat_width),
        attn_total[0],
        attn_total[1],
        attn_total[2],
        attn_total[3],
        attn_total[4],
        attn_total[5],
        attn_total[6],
        attn_total[7],
        mlp_total[0],
        mlp_total[1],
        mlp_total[2],
        mlp_total[3],
        mlp_total[4],
        mlp_total[5],
        mlp_total[6],
    )


def solution(mesh):
    return jax.shard_map(
        per_device,
        mesh=mesh,
        in_specs=(
            P(("rep", "shard"), "seq", None),
            P(("rep", "shard"), None),
            P(("rep", "shard"), "seq", None),
            P(("shard", "seq")),
            P(("shard", "seq")),
            P(("shard", "seq"), None),
            P(("shard", "seq")),
            P(("shard", "seq")),
            P(("shard", "seq"), None),
            P(("shard", "seq")),
            P(("shard", "seq")),
            P(("shard", "seq")),
            P(("shard", "seq")),
            P(("shard", "seq"), None),
            P(("shard", "seq")),
            P(("shard", "seq"), None),
            P(("shard", "seq")),
            P(("shard", "seq")),
        ),
        out_specs=(
            P(("rep", "shard"), "seq", None),
            P(("rep", "shard"), "seq", None),
            P(("shard", "seq")),
            P(("shard", "seq")),
            P(("shard", "seq"), None),
            P(("shard", "seq")),
            P(("shard", "seq")),
            P(("shard", "seq"), None),
            P(("shard", "seq")),
            P(("shard", "seq")),
            P(("shard", "seq")),
            P(("shard", "seq")),
            P(("shard", "seq"), None),
            P(("shard", "seq")),
            P(("shard", "seq"), None),
            P(("shard", "seq")),
            P(("shard", "seq")),
        ),
        check_vma=False,
    )
```

profile of v0, /device:TPU:0, one launch (start us, length us, event | category | flops | bytes accessed | tf_op | source)
XLA Modules:
  0.0 988.8 jit_solution(8182518064212682640)
XLA Ops:
  10.2 13.4 %all-gather.8 = bf16[8,1,128]{2,1,0:T(2,128)(2,1)S(1)} all-gather(bf16[1,1,128]{2,1,0:T(2,128)(2,1)S(1)} %bitcast.164), channel_id=1, replica_groups=mesh['rep'=4,'shard'=4,'seq'=2] {'shard','seq'}, dimensions={0}, use_global_device_ids=true | all-gather | bytes 2304 | tf_op jit(solution)/shard_map/all_gather | solution.py:135
  23.6 8.7 all-gather.2
  32.3 10.8 %all-gather.7 = bf16[8,1,128]{2,1,0:T(2,128)(2,1)S(1)} all-gather(bf16[1,1,128]{2,1,0:T(2,128)(2,1)S(1)} %bitcast.166), channel_id=1, replica_groups=mesh['rep'=4,'shard'=4,'seq'=2] {'shard','seq'}, dimensions={0}, use_global_device_ids=true | all-gather | bytes 2304 | tf_op jit(solution)/shard_map/all_gather | solution.py:88
  43.1 8.8 all-gather.4
  52.0 9.9 %all-gather.3 = bf16[8,1,128]{2,1,0:T(2,128)(2,1)S(1)} all-gather(bf16[1,1,128]{2,1,0:T(2,128)(2,1)S(1)} %bitcast.168), channel_id=1, replica_groups=mesh['rep'=4,'shard'=4,'seq'=2] {'shard','seq'}, dimensions={0}, use_global_device_ids=true | all-gather | bytes 2304 | tf_op jit(solution)/shard_map/all_gather | solution.py:82
  61.9 8.9 all-gather.6
  70.8 10.6 %all-gather.5 = bf16[8,1,128]{2,1,0:T(2,128)(2,1)S(1)} all-gather(bf16[1,1,128]{2,1,0:T(2,128)(2,1)S(1)} %bitcast.170), channel_id=1, replica_groups=mesh['rep'=4,'shard'=4,'seq'=2] {'shard','seq'}, dimensions={0}, use_global_device_ids=true | all-gather | bytes 2304 | tf_op jit(solution)/shard_map/all_gather | solution.py:86
  81.4 8.7 all-gather.9
  90.2 12.8 %all-gather.11 = bf16[8,1,512]{2,1,0:T(2,128)(2,1)S(1)} all-gather(bf16[1,1,512]{2,1,0:T(2,128)(2,1)S(1)} %reshape.245), channel_id=1, replica_groups=mesh['rep'=4,'shard'=4,'seq'=2] {'shard','seq'}, dimensions={0}, use_global_device_ids=true | all-gather | bytes 9216 | tf_op jit(solution)/shard_map/all_gather | solution.py:132
  103.1 9.3 all-gather.10
  112.4 9.5 all-gather.12
  122.3 4.0 fusion.44
  126.5 2.2 all-gather
  129.7 2.3 all-gather.1
  132.3 1.7 fusion.50
  134.7 1.3 convolution_convert_fusion.1
  136.0 3.0 fusion.46
  139.1 51.0 %all-gather.22.cloned.1.call-done = bf16[1024,4096]{1,0:T(8,128)(2,1)} async-done(((bf16[128,4096]{1,0:T(8,128)(2,1)}), bf16[1024,4096]{1,0:T(8,128)(2,1)}) %all-gather.22.cloned.1.call-update) | async-done | bytes 8388624 | tf_op jit(solution)/shard_map/all_gather | solution.py:131
  190.2 6.1 convolution_add_fusion
  196.2 76.0 %all-gather.24.cloned.1.call-done = bf16[4096,1024]{1,0:T(8,128)(2,1)} async-done(((bf16[512,1024]{1,0:T(8,128)(2,1)}), bf16[4096,1024]{1,0:T(8,128)(2,1)}) %all-gather.24.cloned.1.call-update) | async-done | bytes 8388624 | tf_op jit(solution)/shard_map/all_gather | solution.py:133
  272.2 7.2 fusion.51
  279.5 3.0 multiply_reduce_fusion.1
  282.6 1.3 copy-done.3
  283.9 2.5 fusion.25
  286.4 1.5 convolution_convert_fusion
  287.9 1.8 copy.50
  289.7 2.5 fusion.34
  292.5 2.0 multiply_reduce_fusion
  296.3 1.3 convolution_multiply_fusion.1
  297.7 2.7 fusion.40
  302.3 1.4 fusion.48
  303.7 8.3 reduce-scatter.7.cloned.1.call-done
  313.0 6.4 fusion.32
  319.6 1.1 copy-done.12
  320.7 8.2 fusion.28
  329.0 1.5 copy-done.2
  330.5 8.2 fusion.37
  338.7 26.7 %reduce-scatter.13.cloned.1.call-done = f32[128,1024]{1,0:T(8,128)} async-done(((f32[1024,1024]{1,0:T(8,128)}), f32[128,1024]{1,0:T(8,128)}) %reduce-scatter.13.cloned.1.call-update) | async-done | bytes 524304 | tf_op jit(solution)/shard_map/reduce_scatter | solution.py:227
  365.5 129.7 %reduce-scatter.11.cloned.1.call-done = f32[128,3072]{1,0:T(8,128)} async-done(((f32[1024,3072]{1,0:T(8,128)}), f32[128,3072]{1,0:T(8,128)}) %reduce-scatter.11.cloned.1.call-update) | async-done | bytes 1572880 | tf_op jit(solution)/shard_map/reduce_scatter | solution.py:224
  495.2 169.0 %reduce-scatter.15.cloned.1.call-done = f32[128,4096]{1,0:T(8,128)} async-done(((f32[1024,4096]{1,0:T(8,128)}), f32[128,4096]{1,0:T(8,128)}) %reduce-scatter.15.cloned.1.call-update) | async-done | bytes 2097168 | tf_op jit(solution)/shard_map/reduce_scatter | solution.py:169
  664.1 168.8 %reduce-scatter.17.cloned.1.call-done = f32[512,1024]{1,0:T(8,128)} async-done(((f32[4096,1024]{1,0:T(8,128)}), f32[512,1024]{1,0:T(8,128)}) %reduce-scatter.17.cloned.1.call-update) | async-done | bytes 2097168 | tf_op jit(solution)/shard_map/reduce_scatter | solution.py:171
  835.6 5.1 fusion.23
  840.7 26.4 %all-reduce.11 = (f32[1024]{0:T(1024)S(1)}, f32[1024]{0:T(1024)S(1)}, f32[1024]{0:T(1024)S(1)}, f32[1024]{0:T(1024)S(1)}, f32[1024]{0:T(1024)S(1)}, /*index=5*/f...) all-reduce(f32[1024]{0:T(1024)S(1)} %get-tuple-element.19, ...), channel_id=6, replica_groups=mesh['rep'=4,'shard'=4,'seq'=2] {'shard','seq'}, use_global_device_ids=true, to_apply=%region_14.15.clone | all-reduce | flops 14336 | bytes 114688
  868.0 10.9 %all-reduce.12 = (f32[128]{0:T(128)}, f32[128]{0:T(128)}, f32[128]{0:T(128)}, f32[128]{0:T(128)}, f32[128]{0:T(128)}, /*index=5*/f32[128]{0:T(128)}, f32[128]{0:...) all-reduce(f32[128]{0:T(128)S(1)} %dynamic-slice.1, ...), channel_id=1, replica_groups=mesh['rep'=4,'shard'=4,'seq'=2] {'rep'}, use_global_device_ids=true, to_apply=%region_15.16 | all-reduce | flops 1792 | bytes 14336 | tf_op jit(solution)/shard_map/psum | solution.py:231
  879.9 95.1 %all-reduce.16.cloned.1.call-done = (f32[128,3072]{1,0:T(8,128)}, f32[128,1024]{1,0:T(8,128)}, f32[128,4096]{1,0:T(8,128)}, f32[512,1024]{1,0:T(8,128)}) async-done(((f32[128,3072]{1,0:T(8,128)}, f32[128,1024]{1,0:T(8,128)}, f32[128,4096]{1,0:T(8,128)}, f32[512,1024]{1,0:T(8,128)}), (f32[128,3072]{1,0:T(8,128)}, f32[128,1024]{1,0:T(8,128)}, f32[128,4096]{1,0:T(8,128)}, ...) | async-done | bytes 6291472 | tf_op jit(solution)/shard_map/psum | solution.py:231
  975.0 2.9 copy.55
  978.6 1.3 copy.57
  981.0 1.3 copy.58
  (148 shorter events, 15.9 us)
Async XLA Ops:
  7.2 3.0 copy-start.27
  7.2 16.4 %copy-start.28 = (bf16[128]{0:T(256)(128)(2,1)S(1)}, bf16[128]{0:T(256)(128)(2,1)}, u32[]{:S(2)}) copy-start(bf16[128]{0:T(256)(128)(2,1)} %param.28) | copy-start | bytes 772
  7.2 25.1 %copy-start.29 = (bf16[128]{0:T(256)(128)(2,1)S(1)}, bf16[128]{0:T(256)(128)(2,1)}, u32[]{:S(2)}) copy-start(bf16[128]{0:T(256)(128)(2,1)} %param.27) | copy-start | bytes 772
  7.2 35.9 %copy-start.30 = (bf16[128]{0:T(256)(128)(2,1)S(1)}, bf16[128]{0:T(256)(128)(2,1)}, u32[]{:S(2)}) copy-start(bf16[128]{0:T(256)(128)(2,1)} %param.22) | copy-start | bytes 772
  7.2 44.7 %copy-start.31 = (bf16[128]{0:T(256)(128)(2,1)S(1)}, bf16[128]{0:T(256)(128)(2,1)}, u32[]{:S(2)}) copy-start(bf16[128]{0:T(256)(128)(2,1)} %param.21) | copy-start | bytes 772
  7.2 54.7 %copy-start.32 = (bf16[128]{0:T(256)(128)(2,1)S(1)}, bf16[128]{0:T(256)(128)(2,1)}, u32[]{:S(2)}) copy-start(bf16[128]{0:T(256)(128)(2,1)} %param.24) | copy-start | bytes 772
  7.3 63.6 %copy-start.33 = (bf16[128]{0:T(256)(128)(2,1)S(1)}, bf16[128]{0:T(256)(128)(2,1)}, u32[]{:S(2)}) copy-start(bf16[128]{0:T(256)(128)(2,1)} %param.25) | copy-start | bytes 772
  7.3 74.2 %copy-start.34 = (bf16[128]{0:T(256)(128)(2,1)S(1)}, bf16[128]{0:T(256)(128)(2,1)}, u32[]{:S(2)}) copy-start(bf16[128]{0:T(256)(128)(2,1)} %param.29) | copy-start | bytes 772
  7.3 82.9 %copy-start.26 = (bf16[512]{0:T(512)(128)(2,1)S(1)}, bf16[512]{0:T(512)(128)(2,1)}, u32[]{:S(2)}) copy-start(bf16[512]{0:T(512)(128)(2,1)} %param.32) | copy-start | bytes 3076
  7.3 95.8 %copy-start.35 = (bf16[128]{0:T(256)(128)(2,1)S(1)}, bf16[128]{0:T(256)(128)(2,1)}, u32[]{:S(2)}) copy-start(bf16[128]{0:T(256)(128)(2,1)} %param.30) | copy-start | bytes 772
  7.3 105.1 %copy-start.36 = (bf16[128]{0:T(256)(128)(2,1)S(1)}, bf16[128]{0:T(256)(128)(2,1)}, u32[]{:S(2)}) copy-start(bf16[128]{0:T(256)(128)(2,1)} %param.34) | copy-start | bytes 772
  7.3 114.6 %copy-start.37 = (s32[1,256]{1,0:T(1,128)S(1)}, s32[1,256]{1,0:T(1,128)}, u32[]{:S(2)}) copy-start(s32[1,256]{1,0:T(1,128)} %param.19) | copy-start | bytes 3076
  7.3 114.6 %copy-start.4 = (bf16[1,128,1024]{2,1,0:T(8,128)(2,1)S(1)}, bf16[1,128,1024]{2,1,0:T(8,128)(2,1)}, u32[]{:S(2)}) copy-start(bf16[1,128,1024]{2,1,0:T(8,128)(2,1)} %param.18) | copy-start | bytes 786436
  7.3 115.0 %all-gather.18.cloned.1.call-start = ((), (), s32[]{:S(2)}) async-start(), calls=%async_computation.6 | async-start | bytes 7077888 | tf_op jit(solution)/shard_map/all_gather | solution.py:84
  8.1 127.9 %all-gather.20.cloned.1.call-start = ((), (), s32[]{:S(2)}) async-start(), calls=%async_computation.7 | async-start | bytes 2359296 | tf_op jit(solution)/shard_map/all_gather | solution.py:87
  8.8 181.3 %all-gather.22.cloned.1.call-start = ((), (), s32[]{:S(2)}) async-start(), calls=%async_computation.8 | async-start | bytes 9437184 | tf_op jit(solution)/shard_map/all_gather | solution.py:131
  9.5 262.7 %all-gather.24.cloned.1.call-start = ((), (), s32[]{:S(2)}) async-start(), calls=%async_computation.9 | async-start | bytes 9437184 | tf_op jit(solution)/shard_map/all_gather | solution.py:133
  10.1 292.1 %reduce-scatter.9.cloned.1.call-start = ((), (), s32[]{:S(2)}) async-start(), calls=%async_computation.11 | async-start | bytes 1572864 | tf_op jit(solution)/shard_map/reduce_scatter | solution.py:207
  128.8 5.8 copy-start.10
  132.3 2.4 copy-start.8
  190.2 82.1 %copy-start.18 = (bf16[1,128,1024]{2,1,0:T(8,128)(2,1)S(1)}, bf16[1,128,1024]{2,1,0:T(8,128)(2,1)}, u32[]{:S(2)}) copy-start(bf16[1,128,1024]{2,1,0:T(8,128)(2,1)} %param.20) | copy-start | bytes 786436
  272.2 7.3 copy-start
  272.2 10.3 %copy-start.17 = (f32[128,1024]{1,0:T(8,128)S(1)}, f32[128,1024]{1,0:T(8,128)}, u32[]{:S(2)}) copy-start(f32[128,1024]{1,0:T(8,128)} %get-tuple-element.70) | copy-start | bytes 1572868
  272.2 10.4 %copy-start.19 = (bf16[1,128,1024]{2,1,0:T(8,128)(2,1)S(1)}, bf16[1,128,1024]{2,1,0:T(8,128)(2,1)}, u32[]{:S(2)}) copy-start(bf16[1,128,1024]{2,1,0:T(8,128)(2,1)} %param.20) | copy-start | bytes 786436
  279.5 3.1 copy-start.11
  279.5 3.1 copy-start.1
  279.5 4.4 copy-start.3
  283.9 2.5 copy-start.7
  292.2 19.7 %reduce-scatter.7.cloned.1.call-start = ((), (), s32[]{:S(2)}) async-start(), calls=%async_computation.10 | async-start | bytes 1572864 | tf_op jit(solution)/shard_map/reduce_scatter | solution.py:206
  294.5 1.8 copy-start.13
  296.3 1.3 copy-start.14
  297.6 67.9 %reduce-scatter.13.cloned.1.call-start = ((), (), s32[]{:S(2)}) async-start(), calls=%async_computation.13 | async-start | bytes 4718592 | tf_op jit(solution)/shard_map/reduce_scatter | solution.py:227
  300.3 1.2 copy-start.6
  300.3 1.4 copy-start.9
  300.3 194.8 %reduce-scatter.11.cloned.1.call-start = ((), (), s32[]{:S(2)}) async-start(), calls=%async_computation.12 | async-start | bytes 14155776 | tf_op jit(solution)/shard_map/reduce_scatter | solution.py:224
  303.7 15.8 %copy-start.21 = (bf16[128,1024]{0,1:T(8,128)(2,1)}, bf16[128,1024]{0,1:T(8,128)(2,1)S(1)}, u32[]{:S(2)}) copy-start(bf16[128,1024]{0,1:T(8,128)(2,1)S(1)} %get-tuple-element.65) | copy-start | bytes 786436
  313.0 6.5 copy-start.23
  319.5 1.2 copy-start.12
  319.5 344.6 %reduce-scatter.15.cloned.1.call-start = ((), (), s32[]{:S(2)}) async-start(), calls=%async_computation.14 | async-start | bytes 18874368 | tf_op jit(solution)/shard_map/reduce_scatter | solution.py:169
  328.9 1.6 copy-start.2
  328.9 1.6 copy-start.20
  328.9 504.1 %reduce-scatter.17.cloned.1.call-start = ((), (), s32[]{:S(2)}) async-start(), calls=%async_computation.15 | async-start | bytes 18874368 | tf_op jit(solution)/shard_map/reduce_scatter | solution.py:171
  338.7 636.3 %all-reduce.16.cloned.1.call-start = ((), (), s32[]{:S(2)}) async-start(), calls=%async_computation.16 | async-start | bytes 12582912 | tf_op jit(solution)/shard_map/psum | solution.py:231
  833.0 2.6 copy-start.22
  833.0 2.6 copy-start.24
  975.0 2.9 copy-start.25
  975.0 3.7 copy-start.16
  978.6 2.3 copy-start.15
  (2 other events, 1.6 us)
Sparse Core Ops, SparseCore 0:
  9.8 67.4 all-gather.17
  78.9 27.9 all-gather.19
  108.6 81.5 all-gather.21
  191.6 80.5 all-gather.23
  292.4 7.0 reduce-scatter.8
  302.2 9.6 reduce-scatter.6
  314.2 51.1 reduce-scatter.12
  367.8 127.3 reduce-scatter.10
  497.5 166.5 reduce-scatter.14
  666.3 166.5 reduce-scatter.16
  836.7 138.2 all-reduce.15
where the time goes:
time: 990 us; the launch traced here: 989 us
  waiting for transfers between devices  727 us (73%)
  blocking collectives  153 us (15%)
  matrix products  67.1 us (7%)
  local copies, waits for them, and re-layouts  18.9 us (2%)
  between operations  15.7 us (2%)
    reduce_scatter x1, waiting for transfers between devices, per_device(): lax.psum_scatter(upweight_grad, ('shard', 'seq'), scatter_dimension=0, ti...  169 us
    reduce_scatter x1, waiting for transfers between devices, per_device(): lax.psum_scatter(downweight_grad, ('shard', 'seq'), scatter_dimension=0,...  169 us
    reduce_scatter x1, waiting for transfers between devices, per_device(): lax.psum_scatter(qkvweight_grad, ('shard', 'seq'), scatter_dimension=0, t...  130 us
    psum x1, waiting for transfers between devices, per_device(): lax.psum((attn_part[0], attn_part[1], attn_part[2], attn_part[3], attn_pa...  95.1 us
    all_gather x1, waiting for transfers between devices, per_device(): lax.all_gather(downweight, ('shard', 'seq'), axis=0, tiled=True)  76 us
    all_gather x1, waiting for transfers between devices, per_device(): lax.all_gather(upweight, ('shard', 'seq'), axis=0, tiled=True)  51 us
    reduce_scatter x1, waiting for transfers between devices, per_device(): lax.psum_scatter(projweight_grad, ('shard', 'seq'), scatter_dimension=0,...  26.7 us
    unnamed x1, blocking collectives  26.4 us
  transfers between devices with their start and end apart: 11, of which 8 were waited for; matrix products, arithmetic and copies ran while one was open for 6% of the time, Pallas kernels for 0%

commit v1 on v0

--- a/solution.py
+++ b/solution.py
@@ -1,3 +1,5 @@
+import functools
+
 import jax
 import jax.numpy as jnp
 from jax import lax
@@ -262,9 +264,234 @@
     )
 
 
+GROUP = ("shard", "seq")
+
+
+def gather_rows(array):
+    return lax.all_gather(array, GROUP, axis=0, tiled=True)
+
+
+def scatter_rows(array):
+    return lax.psum_scatter(
+        array.astype(jnp.bfloat16), GROUP, scatter_dimension=0, tiled=True
+    ).astype(jnp.float32)
+
+
+def tensor_parallel(shards, seqs, *arguments):
+    (
+        tokens,
+        key_valid,
+        cotangent,
+        attngain,
+        attnshift,
+        qkvweight,
+        querybias,
+        valuebias,
+        projweight,
+        projbias,
+        attnscale,
+        mlpgain,
+        mlpshift,
+        upweight,
+        upbias,
+        downweight,
+        downbias,
+        mlpscale,
+    ) = arguments
+    group = shards * seqs
+    images, tok_rows, width = tokens.shape
+    rows = images * tok_rows
+    own = width // group
+    length = key_valid.shape[1]
+    group_images = shards * images
+    own_heads = HEADS // group
+
+    small = jnp.concatenate(
+        [
+            attngain,
+            attnshift,
+            projbias,
+            attnscale,
+            mlpgain,
+            mlpshift,
+            downbias,
+            mlpscale,
+            key_valid.reshape(-1).astype(jnp.bfloat16),
+        ]
+    )
+    small_all = lax.all_gather(small, GROUP, axis=0, tiled=False)
+
+    def vector(at):
+        return small_all[:, at * own : (at + 1) * own].reshape(width).astype(jnp.float32)
+
+    gain_one, shift_one, bias_proj, scale_one, gain_two, shift_two, bias_down, scale_two = [
+        vector(at) for at in range(8)
+    ]
+    valid = small_all[:, 8 * own :].reshape(shards, seqs, images, length)[:, 0]
+    valid = valid.reshape(group_images, length)
+
+    def to_images(matrix):
+        matrix = matrix.reshape(shards, seqs, images, tok_rows, own_heads, HEAD)
+        return matrix.transpose(0, 2, 1, 3, 4, 5).reshape(group_images, length, own_heads, HEAD)
+
+    def from_images(heads):
+        heads = heads.reshape(shards, images, seqs, tok_rows, own)
+        return heads.transpose(0, 2, 1, 3, 4).reshape(group * rows, own)
+
+    def to_columns(weight, parts):
+        split = weight.reshape(own, parts, group, -1)
+        moved = lax.all_to_all(split, GROUP, split_axis=2, concat_axis=0, tiled=True)
+        return moved.reshape(width, -1)
+
+    def to_rows(grad, parts):
+        split = grad.reshape(width, parts, 1, -1)
+        moved = lax.all_to_all(split, GROUP, split_axis=0, concat_axis=2, tiled=True)
+        return moved.reshape(own, -1)
+
+    tokens_local = tokens.reshape(rows, width)
+    tokens_all = gather_rows(tokens_local)
+    qkv_own = to_columns(qkvweight, 3)
+    up_own = to_columns(upweight, 1)
+    cot_all = gather_rows(cotangent.reshape(rows, width))
+
+    normed_one_all, _ = norm_forward(tokens_all.astype(jnp.float32))
+    act_one = (normed_one_all * gain_one + shift_one).astype(jnp.bfloat16)
+    mixed = jnp.dot(act_one, qkv_own, preferred_element_type=jnp.float32)
+    query_heads = to_images((mixed[:, :own] + querybias.astype(jnp.float32)).astype(jnp.bfloat16))
+    key_heads = to_images(mixed[:, own : 2 * own].astype(jnp.bfloat16))
+    value_heads = to_images(
+        (mixed[:, 2 * own :] + valuebias.astype(jnp.float32)).astype(jnp.bfloat16)
+    )
+    scores = score_block(query_heads, key_heads, valid)
+    top_score = jnp.max(scores, axis=-1, keepdims=True)
+    log_total = top_score + jnp.log(jnp.sum(jnp.exp(scores - top_score), axis=-1, keepdims=True))
+    probs = jnp.exp(scores - log_total)
+    prob_low = probs.astype(jnp.bfloat16)
+    attended = from_images(
+        jnp.einsum(
+            "ihqk,ikhe->iqhe", prob_low, value_heads, preferred_element_type=jnp.float32
+        ).astype(jnp.bfloat16)
+    )
+    branch_one = (
+        scatter_rows(jnp.dot(attended, projweight, preferred_element_type=jnp.float32)) + bias_proj
+    )
+    hidden = tokens_local.astype(jnp.float32)
+    normed_one, spread_one = norm_forward(hidden)
+    middle = hidden + scale_one * branch_one
+    normed_two, spread_two = norm_forward(middle)
+    act_two = gather_rows((normed_two * gain_two + shift_two).astype(jnp.bfloat16))
+
+    inner_pre = jnp.dot(act_two, up_own, preferred_element_type=jnp.float32) + upbias.astype(
+        jnp.float32
+    )
+    activated, gelu_slope = gelu_pair(inner_pre)
+    act_three = activated.astype(jnp.bfloat16)
+    branch_low = (cot_all.astype(jnp.float32) * scale_two).astype(jnp.bfloat16)
+    inner_grad = times_transposed(branch_low, downweight) * gelu_slope
+    inner_low = inner_grad.astype(jnp.bfloat16)
+    acttwo_grad = scatter_rows(times_transposed(inner_low, up_own))
+    branch_two = (
+        scatter_rows(jnp.dot(act_three, downweight, preferred_element_type=jnp.float32)) + bias_down
+    )
+    upbias_grad = jnp.sum(inner_grad, axis=0)
+    downweight_grad = contract_rows(act_three, branch_low).astype(jnp.bfloat16)
+    upweight_grad = contract_rows(act_two, inner_low).astype(jnp.bfloat16)
+    out_grad = cotangent.reshape(rows, width).astype(jnp.float32)
+    middle_grad = out_grad + norm_backward(acttwo_grad * gain_two, normed_two, spread_two)
+    branchone_grad = middle_grad * scale_one
+    proj_low = gather_rows(branchone_grad.astype(jnp.bfloat16))
+
+    block_out = middle + scale_two * branch_two
+
+    back_heads = to_images(times_transposed(proj_low, projweight).astype(jnp.bfloat16))
+    projweight_grad = contract_rows(attended, proj_low).astype(jnp.bfloat16)
+    prob_grad = jnp.einsum(
+        "iqhe,ikhe->ihqk", back_heads, value_heads, preferred_element_type=jnp.float32
+    )
+    row_dot = jnp.sum(probs * prob_grad, axis=-1, keepdims=True)
+    score_low = (probs * (prob_grad - row_dot)).astype(jnp.bfloat16)
+    query_grad = from_images(
+        jnp.einsum("ihqk,ikhe->iqhe", score_low, key_heads, preferred_element_type=jnp.float32)
+        * SCORE_SCALE
+    )
+    key_grad = from_images(
+        jnp.einsum("ihqk,iqhe->ikhe", score_low, query_heads, preferred_element_type=jnp.float32)
+        * SCORE_SCALE
+    )
+    value_grad = from_images(
+        jnp.einsum("ihqk,iqhe->ikhe", prob_low, back_heads, preferred_element_type=jnp.float32)
+    )
+    mixed_low = jnp.concatenate([query_grad, key_grad, value_grad], axis=1).astype(jnp.bfloat16)
+    actone_part = times_transposed(mixed_low, qkv_own)
+    actone_grad = scatter_rows(actone_part)
+    qkvweight_grad = contract_rows(act_one, mixed_low).astype(jnp.bfloat16)
+    tokens_grad = middle_grad + norm_backward(actone_grad * gain_one, normed_one, spread_one)
+
+    vectors = jnp.stack(
+        [
+            jnp.sum(actone_part * normed_one_all, axis=0),
+            jnp.sum(actone_part, axis=0),
+            jnp.sum(branchone_grad, axis=0),
+            jnp.sum(middle_grad * branch_one, axis=0),
+            jnp.sum(acttwo_grad * normed_two, axis=0),
+            jnp.sum(acttwo_grad, axis=0),
+            jnp.sum(out_grad * scale_two, axis=0),
+            jnp.sum(out_grad * branch_two, axis=0),
+        ]
+    )
+    place = lax.axis_index(GROUP)
+    biases = jnp.concatenate(
+        [jnp.sum(query_grad, axis=0), jnp.sum(value_grad, axis=0), upbias_grad]
+    ).reshape(-1)
+    bias_slots = lax.dynamic_update_slice(
+        jnp.zeros((group, biases.shape[0]), jnp.float32), biases[None], (place, 0)
+    )
+    totals = lax.psum(
+        jnp.concatenate([vectors.reshape(-1), bias_slots.reshape(-1)]), ("rep",) + GROUP
+    )
+    vectors = totals[: 8 * width].reshape(8, width)
+    vectors = lax.dynamic_slice(vectors, (0, place * own), (8, own))
+    biases = lax.dynamic_slice(
+        totals[8 * width :].reshape(group, -1), (place, 0), (1, biases.shape[0])
+    )[0]
+
+    downweight_grad, upweight_grad = lax.psum((downweight_grad, upweight_grad), "rep")
+    upweight_grad = to_rows(upweight_grad, 1)
+    upweight_grad, projweight_grad, qkvweight_grad = lax.optimization_barrier(
+        (upweight_grad, projweight_grad, qkvweight_grad)
+    )
+    projweight_grad, qkvweight_grad = lax.psum((projweight_grad, qkvweight_grad), "rep")
+    qkvweight_grad = to_rows(qkvweight_grad, 3)
+
+    return (
+        block_out.reshape(images, tok_rows, width),
+        tokens_grad.reshape(images, tok_rows, width),
+        vectors[0],
+        vectors[1],
+        qkvweight_grad.astype(jnp.float32),
+        biases[:own],
+        biases[own : 2 * own],
+        projweight_grad.astype(jnp.float32),
+        vectors[2],
+        vectors[3],
+        vectors[4],
+        vectors[5],
+        upweight_grad.astype(jnp.float32),
+        biases[2 * own :],
+        downweight_grad.astype(jnp.float32),
+        vectors[6],
+        vectors[7],
+    )
+
+
 def solution(mesh):
+    shards, seqs = mesh.shape["shard"], mesh.shape["seq"]
+    if HEADS % (shards * seqs) == 0:
+        body = functools.partial(tensor_parallel, shards, seqs)
+    else:
+        body = per_device
     return jax.shard_map(
-        per_device,
+        body,
         mesh=mesh,
         in_specs=(
             P(("rep", "shard"), "seq", None),

time: 990 us -> 557 us (0.56)
  waiting for transfers between devices: 727 us -> 316 us
  blocking collectives: 153 us -> 103 us
  matrix products: 67.1 us -> 41.2 us
  starting transfers between devices: 0.66 us -> 20.6 us
  local copies, waits for them, and re-layouts: 18.9 us -> 38.1 us
  other arithmetic: 5.7 us -> 22.6 us
    reduce_scatter x6 -> x4, waiting for transfers between devices: 503 us -> 97.9 us  [scatter_rows(): lax.psum_scatter(array.astype(jnp.bfloat16), GROUP, scatter_dimension=0,...]
    all_gather x4, waiting for transfers between devices: 127 us -> 20.8 us  [gather_rows(): return lax.all_gather(array, GROUP, axis=0, tiled=True)]
    all_to_all x0 -> x4, waiting for transfers between devices: none -> 79.5 us  [the longest x2 42.2 us: to_columns(): lax.all_to_all(split, GROUP, split_axis=2, concat_axis=0, tiled=True)]
    all_gather x13 -> x1, blocking collectives: 116 us -> 41.9 us  [tensor_parallel(): small_all = lax.all_gather(small, GROUP, axis=0, tiled=False)]
    psum x1, blocking collectives: 10.9 us -> 60.9 us  [tensor_parallel(): lax.psum(jnp.concatenate([vectors.reshape(-1), bias_slots.reshape(-1)]),...]
    unnamed x1 -> x0, blocking collectives: 26.4 us -> none
    psum x1 -> x2, waiting for transfers between devices: 95.1 us -> 116 us  [the longest x1 64.8 us: tensor_parallel(): lax.psum((projweight_grad, qkvweight_grad), 'rep')]
    all_to_all x0 -> x4, starting transfers between devices: none -> 19.8 us  [the longest x2 10.6 us: to_columns(): lax.all_to_all(split, GROUP, split_axis=2, concat_axis=0, tiled=True)]
  transfers between devices with their start and end apart: 11 -> 14, of which waited for: 8 -> 8; matrix products, arithmetic and copies ran while one was open for 6% -> 11% of each run, Pallas kernels for 0% -> 0%
where the time goes in v1:
time: 557 us; the launch traced here: 556 us
  waiting for transfers between devices  316 us (57%)
  blocking collectives  103 us (18%)
  matrix products  41.2 us (7%)
  local copies, waits for them, and re-layouts  38.1 us (7%)
  other arithmetic  22.6 us (4%)
  starting transfers between devices  20.6 us (4%)
  between operations  15 us (3%)
    reduce_scatter x4, waiting for transfers between devices, scatter_rows(): lax.psum_scatter(array.astype(jnp.bfloat16), GROUP, scatter_dimension=0,...  97.9 us
    psum x1, waiting for transfers between devices, tensor_parallel(): lax.psum((projweight_grad, qkvweight_grad), 'rep')  64.8 us
    psum x1, blocking collectives, tensor_parallel(): lax.psum(jnp.concatenate([vectors.reshape(-1), bias_slots.reshape(-1)]),...  60.9 us
    psum x1, waiting for transfers between devices, tensor_parallel(): lax.psum((downweight_grad, upweight_grad), 'rep')  51.6 us
    all_to_all x2, waiting for transfers between devices, to_columns(): lax.all_to_all(split, GROUP, split_axis=2, concat_axis=0, tiled=True)  42.2 us
    all_gather x1, blocking collectives, tensor_parallel(): small_all = lax.all_gather(small, GROUP, axis=0, tiled=False)  41.9 us
    all_to_all x2, waiting for transfers between devices, to_rows(): lax.all_to_all(split, GROUP, split_axis=0, concat_axis=2, tiled=True)  37.3 us
    all_gather x4, waiting for transfers between devices, gather_rows(): return lax.all_gather(array, GROUP, axis=0, tiled=True)  20.8 us
  transfers between devices with their start and end apart: 14, of which 8 were waited for; matrix products, arithmetic and copies ran while one was open for 11% of the time, Pallas kernels for 0%

profile of v1, /device:TPU:0, one launch (start us, length us, event | category | flops | bytes accessed | tf_op | source)
XLA Modules:
  0.0 556.3 jit_solution(3729402814858712403)
XLA Ops:
  8.1 1.6 copy.158
  10.6 6.3 %all-to-all-start = ((bf16[128,3,8,128]{0,3,1,2:T(8,128)(2,1)}), bf16[128,3,8,128]{0,3,1,2:T(8,128)(2,1)S(1)}, u32[]{:S(2)}, u32[]{:S(2)}) async-start(bf16[128,3,8,128]{0,3,1,2:T(8,128)(2,1)} %copy.159), calls=%async_computation | async-start | bytes 1572864 | tf_op jit(solution)/shard_map/all_to_all | solution.py:343
  18.8 41.9 %all-gather.3 = bf16[8,1,1280]{2,1,0:T(2,128)(2,1)S(1)} all-gather(bf16[1,1,1280]{2,1,0:T(2,128)(2,1)S(1)} %reshape.266), channel_id=2, replica_groups=mesh['rep'=4,'shard'=4,'seq'=2] {'shard','seq'}, dimensions={0}, use_global_device_ids=true | all-gather | bytes 23040 | tf_op jit(solution)/shard_map/all_gather | solution.py:322
  61.3 2.2 convert_reduce_fusion
  65.4 1.3 fusion.32
  69.9 1.7 fusion.76
  73.3 2.1 convolution_convert_fusion.2
  75.4 35.1 %reduce-scatter.5.cloned.1.call-done = bf16[128,1024]{1,0:T(8,128)(2,1)} async-done(((bf16[1024,1024]{1,0:T(8,128)(2,1)}), bf16[128,1024]{1,0:T(8,128)(2,1)}) %reduce-scatter.5.cloned.1.call-update) | async-done | bytes 262160 | tf_op jit(solution)/shard_map/reduce_scatter | solution.py:275
  110.5 1.1 fusion.72
  111.6 1.2 multiply_reduce_fusion.2
  112.8 1.8 add_convert_fusion
  115.3 2.3 copy.169
  117.5 4.3 all-to-all-start.1
  122.1 42.2 %all-to-all-done.1 = bf16[128,1,8,512]{0,3,1,2:T(8,128)(2,1)} async-done(((bf16[128,1,8,512]{0,3,1,2:T(8,128)(2,1)}), bf16[128,1,8,512]{0,3,1,2:T(8,128)(2,1)}, u32[]{:S(2)}, u32[]{:S(2)}) %all-to-all-start.1) | async-done | bytes 1048608 | tf_op jit(solution)/shard_map/all_to_all | solution.py:343
  164.3 2.3 copy.171
  166.6 5.0 multiply_convert_fusion.1
  171.5 20.7 %all-gather.15.cloned.1.call-done = bf16[1,1024,1024]{2,1,0:T(8,128)(2,1)} async-done(((bf16[1,128,1024]{2,1,0:T(8,128)(2,1)}), bf16[1,1024,1024]{2,1,0:T(8,128)(2,1)}) %all-gather.15.cloned.1.call-update) | async-done | bytes 2097168 | tf_op jit(solution)/shard_map/all_gather | solution.py:271
  192.3 4.1 fusion.77
  197.4 2.6 convolution_convert_fusion
  200.1 3.8 convolution_convert_fusion.1
  204.1 4.3 fusion.23
  208.5 27.0 %reduce-scatter.9.cloned.1.call-done = bf16[128,1024]{1,0:T(8,128)(2,1)} async-done(((bf16[1024,1024]{1,0:T(8,128)(2,1)}), bf16[128,1024]{1,0:T(8,128)(2,1)}) %reduce-scatter.9.cloned.1.call-update) | async-done | bytes 262160 | tf_op jit(solution)/shard_map/reduce_scatter | solution.py:275
  235.5 1.4 fusion.54
  237.0 35.8 %reduce-scatter.7.cloned.1.call-done = bf16[128,1024]{1,0:T(8,128)(2,1)} async-done(((bf16[1024,1024]{1,0:T(8,128)(2,1)}), bf16[128,1024]{1,0:T(8,128)(2,1)}) %reduce-scatter.7.cloned.1.call-update) | async-done | bytes 262160 | tf_op jit(solution)/shard_map/reduce_scatter | solution.py:275
  272.7 2.4 multiply_reduce_fusion.1
  276.0 51.6 %all-reduce.4.cloned.1.call-done = bf16[1024,1,1,512]{3,0,2,1:T(8,128)(2,1)} async-done(((bf16[1024,1,1,512]{3,0,2,1:T(8,128)(2,1)}), bf16[1024,1,1,512]{3,0,2,1:T(8,128)(2,1)}) %all-reduce.4.cloned.1.call-update) | async-done | bytes 1048592 | tf_op jit(solution)/shard_map/psum | solution.py:458
  328.1 3.3 reduce.6
  331.4 2.6 reshape.274
  334.0 4.6 all-to-all-start.2
  338.9 4.2 fusion.20
  343.1 37.3 %all-to-all-done.2 = bf16[8,2,32768]{2,1,0:T(2,128)(2,1)S(1)} async-done(((bf16[8,2,32768]{2,1,0:T(2,128)(2,1)}), bf16[8,2,32768]{2,1,0:T(2,128)(2,1)S(1)}, u32[]{:S(2)}, u32[]{:S(2)}) %all-to-all-start.2) | async-done | bytes 1048608 | tf_op jit(solution)/shard_map/all_to_all | solution.py:348
  380.4 3.4 reshape.275
  383.8 1.9 copy.204
  385.7 1.3 copy.185
  387.0 2.3 convolution_convert_fusion.6
  394.6 2.2 convolution_convert_fusion.4
  396.9 1.2 convolution_convert_fusion.5
  398.0 2.4 copy.186
  400.6 4.2 fusion.73
  404.7 64.8 %all-reduce.6.cloned.1.call-done = (bf16[1024,3,1,128]{0,3,1,2:T(8,128)(2,1)}, bf16[128,1024]{1,0:T(8,128)(2,1)}, bf16[512,1024]{1,0:T(8,128)(2,1)}) async-done(((bf16[1024,3,1,128]{0,3,1,2:T(8,128)(2,1)}, bf16[128,1024]{1,0:T(8,128)(2,1)}, bf16[512,1024]{1,0:T(8,128)(2,1)}), (bf16[1024,3,1,128]{0,3,1,2:T(8,128)(2,1)}, bf16[128,1024]{1,0:T(8,128)(2,1)}, ...) | async-done | bytes 2097168 | tf_op jit(solution)/shard_map/psum | solution.py:463
  469.6 2.4 copy.187
  472.0 4.6 all-to-all-start.3
  477.0 60.9 %psum.35 = f32[14336]{0:T(1024)S(1)} all-reduce(f32[14336]{0:T(1024)S(1)} %pad_maximum_fusion), channel_id=1, replica_groups=mesh['rep'=4,'shard'=4,'seq'=2] {'rep','shard','seq'}, use_global_device_ids=true, to_apply=%region_28.29 | all-reduce | flops 14336 | bytes 114688 | tf_op jit(solution)/shard_map/psum | solution.py:449
  538.0 1.6 copy.189
  541.4 1.6 convert_element_type.261
  544.9 1.4 reshape.257
  546.3 1.2 fusion.59
  547.5 2.0 fusion.49
  (191 shorter events, 23.9 us)
Async XLA Ops:
  7.2 185.1 %copy-start = (bf16[512,1024]{1,0:T(8,128)(2,1)S(1)}, bf16[512,1024]{1,0:T(8,128)(2,1)}, u32[]{:S(2)}) copy-start(bf16[512,1024]{1,0:T(8,128)(2,1)} %param.33) | copy-start | bytes 3145732
  7.2 54.1 %all-gather.13.cloned.1.call-start = ((), (), s32[]{:S(2)}) async-start(), calls=%async_computation.15 | async-start | bytes 2359296 | tf_op jit(solution)/shard_map/all_gather | solution.py:271
  7.9 9.0 %copy-start.27 = (bf16[128]{0:T(256)(128)(2,1)S(1)}, bf16[128]{0:T(256)(128)(2,1)}, u32[]{:S(2)}) copy-start(bf16[128]{0:T(256)(128)(2,1)} %param.21) | copy-start | bytes 772
  8.0 9.3 %copy-start.28 = (bf16[128]{0:T(256)(128)(2,1)S(1)}, bf16[128]{0:T(256)(128)(2,1)}, u32[]{:S(2)}) copy-start(bf16[128]{0:T(256)(128)(2,1)} %param.22) | copy-start | bytes 772
  8.0 9.5 %copy-start.29 = (bf16[128]{0:T(256)(128)(2,1)S(1)}, bf16[128]{0:T(256)(128)(2,1)}, u32[]{:S(2)}) copy-start(bf16[128]{0:T(256)(128)(2,1)} %param.27) | copy-start | bytes 772
  8.0 9.7 %copy-start.30 = (bf16[128]{0:T(256)(128)(2,1)S(1)}, bf16[128]{0:T(256)(128)(2,1)}, u32[]{:S(2)}) copy-start(bf16[128]{0:T(256)(128)(2,1)} %param.28) | copy-start | bytes 772
  8.0 9.9 %copy-start.31 = (bf16[128]{0:T(256)(128)(2,1)S(1)}, bf16[128]{0:T(256)(128)(2,1)}, u32[]{:S(2)}) copy-start(bf16[128]{0:T(256)(128)(2,1)} %param.29) | copy-start | bytes 772
  8.0 10.1 %copy-start.32 = (bf16[128]{0:T(256)(128)(2,1)S(1)}, bf16[128]{0:T(256)(128)(2,1)}, u32[]{:S(2)}) copy-start(bf16[128]{0:T(256)(128)(2,1)} %param.30) | copy-start | bytes 772
  8.0 10.3 %copy-start.33 = (bf16[128]{0:T(256)(128)(2,1)S(1)}, bf16[128]{0:T(256)(128)(2,1)}, u32[]{:S(2)}) copy-start(bf16[128]{0:T(256)(128)(2,1)} %param.34) | copy-start | bytes 772
  8.0 10.5 %copy-start.34 = (bf16[128]{0:T(256)(128)(2,1)S(1)}, bf16[128]{0:T(256)(128)(2,1)}, u32[]{:S(2)}) copy-start(bf16[128]{0:T(256)(128)(2,1)} %param.35) | copy-start | bytes 772
  8.0 10.7 %copy-start.35 = (s32[1,256]{1,0:T(1,128)S(1)}, s32[1,256]{1,0:T(1,128)}, u32[]{:S(2)}) copy-start(s32[1,256]{1,0:T(1,128)} %param.19) | copy-start | bytes 3076
  8.0 52.6 %copy-start.36 = (bf16[128]{0:T(256)(128)(2,1)S(1)}, bf16[128]{0:T(256)(128)(2,1)}, u32[]{:S(2)}) copy-start(bf16[128]{0:T(256)(128)(2,1)} %param.25) | copy-start | bytes 772
  8.0 52.6 %copy-start.37 = (bf16[128]{0:T(256)(128)(2,1)S(1)}, bf16[128]{0:T(256)(128)(2,1)}, u32[]{:S(2)}) copy-start(bf16[128]{0:T(256)(128)(2,1)} %param.24) | copy-start | bytes 772
  10.6 50.2 %all-to-all-start = ((bf16[128,3,8,128]{0,3,1,2:T(8,128)(2,1)}), bf16[128,3,8,128]{0,3,1,2:T(8,128)(2,1)S(1)}, u32[]{:S(2)}, u32[]{:S(2)}) async-start(bf16[128,3,8,128]{0,3,1,2:T(8,128)(2,1)} %copy.159), calls=%async_computation | async-start | bytes 1572864 | tf_op jit(solution)/shard_map/all_to_all | solution.py:343
  16.9 93.6 %reduce-scatter.5.cloned.1.call-start = ((), (), s32[]{:S(2)}) async-start(), calls=%async_computation.8 | async-start | bytes 2359296 | tf_op jit(solution)/shard_map/reduce_scatter | solution.py:275
  61.3 4.1 copy-start.22
  61.3 2.5 copy-start.3
  69.8 2.0 copy-start.10
  71.8 1.4 copy-start.19
  73.3 37.2 %copy-start.2 = (bf16[1,128,1024]{2,1,0:T(8,128)(2,1)S(1)}, bf16[1,128,1024]{2,1,0:T(8,128)(2,1)}, u32[]{:S(2)}) copy-start(bf16[1,128,1024]{2,1,0:T(8,128)(2,1)} %param.18) | copy-start | bytes 786436
  75.3 91.2 %all-gather.9.cloned.1.call-start = ((), (), s32[]{:S(2)}) async-start(), calls=%async_computation.9 | async-start | bytes 2359296 | tf_op jit(solution)/shard_map/all_gather | solution.py:271
  114.7 77.6 %all-gather.15.cloned.1.call-start = ((), (), s32[]{:S(2)}) async-start(), calls=%async_computation.16 | async-start | bytes 2359296 | tf_op jit(solution)/shard_map/all_gather | solution.py:271
  115.3 6.8 %copy-start.26 = (bf16[512]{0:T(512)(128)(2,1)S(1)}, bf16[512]{0:T(512)(128)(2,1)}, u32[]{:S(2)}) copy-start(bf16[512]{0:T(512)(128)(2,1)} %param.32) | copy-start | bytes 3076
  117.5 46.8 %all-to-all-start.1 = ((bf16[128,1,8,512]{0,3,1,2:T(8,128)(2,1)}), bf16[128,1,8,512]{0,3,1,2:T(8,128)(2,1)}, u32[]{:S(2)}, u32[]{:S(2)}) async-start(bf16[128,1,8,512]{0,3,1,2:T(8,128)(2,1)} %bitcast.263), calls=%async_computation.2 | async-start | bytes 2097152 | tf_op jit(solution)/shard_map/all_to_all | solution.py:343
  121.8 113.7 %reduce-scatter.9.cloned.1.call-start = ((), (), s32[]{:S(2)}) async-start(), calls=%async_computation.11 | async-start | bytes 2359296 | tf_op jit(solution)/shard_map/reduce_scatter | solution.py:275
  192.3 5.1 copy-start.20
  200.0 72.7 %reduce-scatter.7.cloned.1.call-start = ((), (), s32[]{:S(2)}) async-start(), calls=%async_computation.10 | async-start | bytes 2359296 | tf_op jit(solution)/shard_map/reduce_scatter | solution.py:275
  203.9 123.7 %all-reduce.4.cloned.1.call-start = ((), (), s32[]{:S(2)}) async-start(), calls=%async_computation.14 | async-start | bytes 2097152 | tf_op jit(solution)/shard_map/psum | solution.py:458
  204.1 31.5 %copy-start.6 = (bf16[128,1024]{1,0:T(8,128)(2,1)S(1)}, bf16[128,1024]{1,0:T(8,128)(2,1)}, u32[]{:S(2)}) copy-start(bf16[128,1024]{1,0:T(8,128)(2,1)} %reduce-scatter.5.cloned.1.call-done) | copy-start | bytes 786436
  204.1 68.7 %copy-start.21 = (bf16[1,128,1024]{2,1,0:T(8,128)(2,1)S(1)}, bf16[1,128,1024]{2,1,0:T(8,128)(2,1)}, u32[]{:S(2)}) copy-start(bf16[1,128,1024]{2,1,0:T(8,128)(2,1)} %param.20) | copy-start | bytes 786436
  208.4 178.6 %all-gather.11.cloned.1.call-start = ((), (), s32[]{:S(2)}) async-start(), calls=%async_computation.12 | async-start | bytes 2359296 | tf_op jit(solution)/shard_map/all_gather | solution.py:271
  275.1 58.9 %copy-start.7 = (f32[128,1024]{1,0:T(8,128)}, f32[128,1024]{1,0:T(8,128)S(1)}, u32[]{:S(2)}) copy-start(f32[128,1024]{1,0:T(8,128)S(1)} %get-tuple-element.56) | copy-start | bytes 1572868
  334.0 46.3 %all-to-all-start.2 = ((bf16[8,2,32768]{2,1,0:T(2,128)(2,1)}), bf16[8,2,32768]{2,1,0:T(2,128)(2,1)S(1)}, u32[]{:S(2)}, u32[]{:S(2)}) async-start(bf16[8,2,32768]{2,1,0:T(2,128)(2,1)} %reshape.274), calls=%async_computation.6 | async-start | bytes 2097152 | tf_op jit(solution)/shard_map/all_to_all | solution.py:348
  338.6 131.0 %all-reduce.6.cloned.1.call-start = ((), (), s32[]{:S(2)}) async-start(), calls=%async_computation.17 | async-start | bytes 4194304 | tf_op jit(solution)/shard_map/psum | solution.py:463
  391.1 1.4 copy-start.15
  393.0 1.6 copy-start.17
  394.6 2.2 copy-start.25
  394.6 2.2 copy-start.5
  394.6 2.2 copy-start.13
  398.0 2.5 copy-start.4
  398.0 2.5 copy-start.23
  400.5 145.8 %reduce-scatter.11.cloned.1.call-start = ((), (), s32[]{:S(2)}) async-start(), calls=%async_computation.13 | async-start | bytes 2359296 | tf_op jit(solution)/shard_map/reduce_scatter | solution.py:275
  469.6 68.4 %copy-start.9 = (bf16[128,1,8,1,512]{0,4,2,3,1:T(8,128)(2,1)S(1)}, bf16[128,1,8,1,512]{0,4,2,3,1:T(8,128)(2,1)}, u32[]{:S(2)}) copy-start(bf16[128,1,8,1,512]{0,4,2,3,1:T(8,128)(2,1)} %copy.185) | copy-start | bytes 3145732
  472.0 71.8 %all-to-all-start.3 = ((bf16[1024,3,1,128]{3,1,2,0:T(4,128)(2,1)}), bf16[1024,3,1,128]{3,1,2,0:T(4,128)(2,1)S(1)}, u32[]{:S(2)}, u32[]{:S(2)}) async-start(bf16[1024,3,1,128]{3,1,2,0:T(4,128)(2,1)} %copy.187), calls=%async_computation.7 | async-start | bytes 2097152 | tf_op jit(solution)/shard_map/all_to_all | solution.py:348
  476.6 64.8 %copy-start.18 = (bf16[512,1024]{1,0:T(8,128)(2,1)S(1)}, bf16[512,1024]{1,0:T(8,128)(2,1)}, u32[]{:S(2)}) copy-start(bf16[512,1024]{1,0:T(8,128)(2,1)} %get-tuple-element.55) | copy-start | bytes 3145732
  539.6 3.4 copy-start.24
  544.0 5.5 copy-start.1
  544.9 2.6 copy-start.8
  (5 other events, 5.1 us)
Sparse Core Ops, SparseCore 0:
  9.6 46.7 all-gather.12
  75.5 34.9 reduce-scatter.4
  114.8 47.7 all-gather.8
  164.0 28.2 all-gather.14
  200.1 35.3 reduce-scatter.8
  238.3 34.4 reduce-scatter.6
  276.4 51.1 all-reduce.3
  329.8 48.4 all-gather.10
  400.6 68.9 all-reduce.5
  471.8 51.5 reduce-scatter.10

commit v2 on v1

--- a/solution.py
+++ b/solution.py
@@ -3,6 +3,8 @@
 import jax
 import jax.numpy as jnp
 from jax import lax
+from jax.experimental import pallas as pl
+from jax.experimental.pallas import tpu as pltpu
 from jax.sharding import PartitionSpec as P
 
 HEADS = 16
@@ -271,10 +273,164 @@
     return lax.all_gather(array, GROUP, axis=0, tiled=True)
 
 
-def scatter_rows(array):
-    return lax.psum_scatter(
-        array.astype(jnp.bfloat16), GROUP, scatter_dimension=0, tiled=True
-    ).astype(jnp.float32)
+VMEM_LIMIT = 40 * 1024 * 1024
+
+
+def chip_barrier(shards, shard, other):
+    barrier = pltpu.get_barrier_semaphore()
+    for step in range(1, shards):
+        pl.semaphore_signal(
+            barrier, inc=1, device_id={"shard": lax.rem(shard + step, shards)}
+        )
+    pl.semaphore_signal(barrier, inc=1, device_id={"seq": other})
+    pl.semaphore_wait(barrier, shards)
+
+
+def gather_kernel(shards, count, *refs):
+    sources, results = refs[:count], refs[count : 2 * count]
+    send_sem, recv_sem, local_sem = refs[2 * count :]
+    shard, seq = lax.axis_index("shard"), lax.axis_index("seq")
+    other = 1 - seq
+    place = 2 * shard + seq
+    chip_barrier(shards, shard, other)
+
+    def push(source, target, slot, device):
+        copy = pltpu.make_async_remote_copy(
+            src_ref=source,
+            dst_ref=target,
+            send_sem=send_sem.at[slot],
+            recv_sem=recv_sem.at[slot],
+            device_id=device,
+        )
+        copy.start()
+        return copy
+
+    slots = 2 * shards - 1
+    along, pending, local = {}, [], []
+    for at in range(count):
+        for step in range(1, shards):
+            along[at, step] = push(
+                sources[at],
+                results[at].at[place],
+                at * slots + step - 1,
+                {"shard": lax.rem(shard + step, shards)},
+            )
+        pending.append(
+            push(sources[at], results[at].at[place], at * slots + shards - 1, {"seq": other})
+        )
+        copy = pltpu.make_async_copy(sources[at], results[at].at[place], local_sem.at[at])
+        copy.start()
+        local.append(copy)
+    for at in range(count):
+        for step in range(1, shards):
+            along[at, step].wait_recv()
+            origin = 2 * lax.rem(shard + shards - step, shards) + seq
+            pending.append(
+                push(
+                    results[at].at[origin],
+                    results[at].at[origin],
+                    at * slots + shards - 1 + step,
+                    {"seq": other},
+                )
+            )
+    for copy in local:
+        copy.wait()
+    for copy in along.values():
+        copy.wait_send()
+    for copy in pending:
+        copy.wait()
+
+
+def gather_group(shards, call, *arrays):
+    count = len(arrays)
+    copies = count * (2 * shards - 1)
+    results = pl.pallas_call(
+        functools.partial(gather_kernel, shards, count),
+        out_shape=[
+            jax.ShapeDtypeStruct((2 * shards,) + array.shape, array.dtype) for array in arrays
+        ],
+        in_specs=[pl.BlockSpec(memory_space=pltpu.VMEM)] * count,
+        out_specs=[pl.BlockSpec(memory_space=pltpu.VMEM)] * count,
+        scratch_shapes=[
+            pltpu.SemaphoreType.DMA((copies,)),
+            pltpu.SemaphoreType.DMA((copies,)),
+            pltpu.SemaphoreType.DMA((count,)),
+        ],
+        compiler_params=pltpu.CompilerParams(
+            collective_id=call, has_side_effects=True, vmem_limit_bytes=VMEM_LIMIT
+        ),
+        name="gather_group_%d" % call,
+    )(*arrays)
+    return results
+
+
+def scatter_kernel(shards, terms, total, near, outgoing, arrived, send_sem, recv_sem):
+    shard, seq = lax.axis_index("shard"), lax.axis_index("seq")
+    other = 1 - seq
+    chip_barrier(shards, shard, other)
+
+    def push(source, target, slot, device):
+        copy = pltpu.make_async_remote_copy(
+            src_ref=source,
+            dst_ref=target,
+            send_sem=send_sem.at[slot],
+            recv_sem=recv_sem.at[slot],
+            device_id=device,
+        )
+        copy.start()
+        return copy
+
+    first, second = [], []
+    for step in range(1, shards + 1):
+        target = lax.rem(shard + step, shards)
+        first.append(
+            push(terms.at[2 * target + other], near.at[step - 1], step - 1, {"seq": other})
+        )
+    for step in range(1, shards + 1):
+        target = lax.rem(shard + step, shards)
+        first[step - 1].wait_recv()
+        both = terms[2 * target + seq].astype(jnp.float32) + near[step - 1].astype(jnp.float32)
+        if step == shards:
+            total[...] = both
+        else:
+            outgoing[step - 1] = both.astype(jnp.bfloat16)
+            second.append(
+                push(
+                    outgoing.at[step - 1],
+                    arrived.at[step - 1],
+                    shards + step - 1,
+                    {"shard": target},
+                )
+            )
+    for step in range(1, shards):
+        second[step - 1].wait_recv()
+        total[...] += arrived[step - 1].astype(jnp.float32)
+    for copy in first + second:
+        copy.wait_send()
+
+
+def scatter_group(shards, call, terms):
+    terms = terms.astype(jnp.bfloat16)
+    rows, columns = terms.shape
+    block = (rows // (2 * shards), columns)
+    copies = 2 * shards - 1
+    return pl.pallas_call(
+        functools.partial(scatter_kernel, shards),
+        out_shape=jax.ShapeDtypeStruct(block, jnp.float32),
+        in_specs=[pl.BlockSpec(memory_space=pltpu.VMEM)],
+        out_specs=pl.BlockSpec(memory_space=pltpu.VMEM),
+        scratch_shapes=[
+            pltpu.VMEM((shards,) + block, jnp.bfloat16),
+            pltpu.VMEM((shards - 1,) + block, jnp.bfloat16),
+            pltpu.VMEM((shards - 1,) + block, jnp.bfloat16),
+            pltpu.SemaphoreType.DMA((copies,)),
+            pltpu.SemaphoreType.DMA((copies,)),
+        ],
+        compiler_params=pltpu.CompilerParams(
+            collective_id=call, has_side_effects=True, vmem_limit_bytes=VMEM_LIMIT
+        ),
+        name="scatter_group_%d" % call,
+    )(terms.reshape((2 * shards,) + block))
 
 
 def tensor_parallel(shards, seqs, *arguments):
@@ -319,7 +475,13 @@
             key_valid.reshape(-1).astype(jnp.bfloat16),
         ]
     )
-    small_all = lax.all_gather(small, GROUP, axis=0, tiled=False)
+    used = small.shape[0]
+    padded = -(-used // 2048) * 2048
+    small = jnp.pad(small, (0, padded - used)).reshape(-1, 128)
+    tokens_local = tokens.reshape(rows, width)
+    tokens_all, small_all = gather_group(shards, 0, tokens_local, small)
+    tokens_all = tokens_all.reshape(group * rows, width)
+    small_all = small_all.reshape(group, padded)
 
     def vector(at):
         return small_all[:, at * own : (at + 1) * own].reshape(width).astype(jnp.float32)
@@ -327,7 +489,7 @@
     gain_one, shift_one, bias_proj, scale_one, gain_two, shift_two, bias_down, scale_two = [
         vector(at) for at in range(8)
     ]
-    valid = small_all[:, 8 * own :].reshape(shards, seqs, images, length)[:, 0]
+    valid = small_all[:, 8 * own : used].reshape(shards, seqs, images, length)[:, 0]
     valid = valid.reshape(group_images, length)
 
     def to_images(matrix):
@@ -348,8 +510,6 @@
         moved = lax.all_to_all(split, GROUP, split_axis=0, concat_axis=2, tiled=True)
         return moved.reshape(own, -1)
 
-    tokens_local = tokens.reshape(rows, width)
-    tokens_all = gather_rows(tokens_local)
     qkv_own = to_columns(qkvweight, 3)
     up_own = to_columns(upweight, 1)
     cot_all = gather_rows(cotangent.reshape(rows, width))
@@ -373,13 +533,15 @@
         ).astype(jnp.bfloat16)
     )
     branch_one = (
-        scatter_rows(jnp.dot(attended, projweight, preferred_element_type=jnp.float32)) + bias_proj
+        scatter_group(shards, 1, jnp.dot(attended, projweight, preferred_element_type=jnp.float32)) + bias_proj
     )
     hidden = tokens_local.astype(jnp.float32)
     normed_one, spread_one = norm_forward(hidden)
     middle = hidden + scale_one * branch_one
     normed_two, spread_two = norm_forward(middle)
-    act_two = gather_rows((normed_two * gain_two + shift_two).astype(jnp.bfloat16))
+    act_two = gather_group(
+        shards, 2, (normed_two * gain_two + shift_two).astype(jnp.bfloat16)
+    )[0].reshape(group * rows, width)
 
     inner_pre = jnp.dot(act_two, up_own, preferred_element_type=jnp.float32) + upbias.astype(
         jnp.float32
@@ -389,9 +551,9 @@
     branch_low = (cot_all.astype(jnp.float32) * scale_two).astype(jnp.bfloat16)
     inner_grad = times_transposed(branch_low, downweight) * gelu_slope
     inner_low = inner_grad.astype(jnp.bfloat16)
-    acttwo_grad = scatter_rows(times_transposed(inner_low, up_own))
+    acttwo_grad = scatter_group(shards, 3, times_transposed(inner_low, up_own))
     branch_two = (
-        scatter_rows(jnp.dot(act_three, downweight, preferred_element_type=jnp.float32)) + bias_down
+        scatter_group(shards, 4, jnp.dot(act_three, downweight, preferred_element_type=jnp.float32)) + bias_down
     )
     upbias_grad = jnp.sum(inner_grad, axis=0)
     downweight_grad = contract_rows(act_three, branch_low).astype(jnp.bfloat16)
@@ -399,7 +561,9 @@
     out_grad = cotangent.reshape(rows, width).astype(jnp.float32)
     middle_grad = out_grad + norm_backward(acttwo_grad * gain_two, normed_two, spread_two)
     branchone_grad = middle_grad * scale_one
-    proj_low = gather_rows(branchone_grad.astype(jnp.bfloat16))
+    proj_low = gather_group(shards, 5, branchone_grad.astype(jnp.bfloat16))[0].reshape(
+        group * rows, width
+    )
 
     block_out = middle + scale_two * branch_two
 
@@ -423,7 +587,7 @@
     )
     mixed_low = jnp.concatenate([query_grad, key_grad, value_grad], axis=1).astype(jnp.bfloat16)
     actone_part = times_transposed(mixed_low, qkv_own)
-    actone_grad = scatter_rows(actone_part)
+    actone_grad = scatter_group(shards, 6, actone_part)
     qkvweight_grad = contract_rows(act_one, mixed_low).astype(jnp.bfloat16)
     tokens_grad = middle_grad + norm_backward(actone_grad * gain_one, normed_one, spread_one)
 
@@ -457,8 +621,8 @@
 
     downweight_grad, upweight_grad = lax.psum((downweight_grad, upweight_grad), "rep")
     upweight_grad = to_rows(upweight_grad, 1)
-    upweight_grad, projweight_grad, qkvweight_grad = lax.optimization_barrier(
-        (upweight_grad, projweight_grad, qkvweight_grad)
+    upweight_grad, downweight_grad, projweight_grad, qkvweight_grad = lax.optimization_barrier(
+        (upweight_grad, downweight_grad, projweight_grad, qkvweight_grad)
     )
     projweight_grad, qkvweight_grad = lax.psum((projweight_grad, qkvweight_grad), "rep")
     qkvweight_grad = to_rows(qkvweight_grad, 3)
@@ -486,7 +650,7 @@
 
 def solution(mesh):
     shards, seqs = mesh.shape["shard"], mesh.shape["seq"]
-    if HEADS % (shards * seqs) == 0:
+    if seqs == 2 and HEADS % (shards * seqs) == 0:
         body = functools.partial(tensor_parallel, shards, seqs)
     else:
         body = per_device

time: 557 us -> 506 us (0.908)
  Pallas kernels: 0 us -> 220 us
  waiting for transfers between devices: 316 us -> 104 us
  blocking collectives: 103 us -> 46.1 us
  local copies, waits for them, and re-layouts: 38.1 us -> 47.4 us
  matrix products: 41.2 us -> 33.2 us
  other arithmetic: 22.6 us -> 15.5 us
    pallas_call x0 -> x7, Pallas kernels: none -> 220 us  [the longest x3 115 us: gather_group(): pl.pallas_call(functools.partial(gather_kernel, shards, count), out_shape...]
    reduce_scatter x4 -> x0, waiting for transfers between devices: 97.9 us -> none  [scatter_rows(): lax.psum_scatter(array.astype(jnp.bfloat16), GROUP, scatter_dimension=0,...]
    all_to_all x2, waiting for transfers between devices: 42.2 us -> 0.01 us  [to_columns(): lax.all_to_all(split, GROUP, split_axis=2, concat_axis=0, tiled=True)]
    all_gather x1 -> x0, blocking collectives: 41.9 us -> none  [tensor_parallel(): small_all = lax.all_gather(small, GROUP, axis=0, tiled=False)]
    all_gather x4 -> x1, waiting for transfers between devices: 20.8 us -> 0.02 us  [gather_rows(): return lax.all_gather(array, GROUP, axis=0, tiled=True)]
    all_to_all x2, waiting for transfers between devices: 37.3 us -> 16.8 us  [to_rows(): lax.all_to_all(split, GROUP, split_axis=0, concat_axis=2, tiled=True)]
    psum x1, waiting for transfers between devices: 51.6 us -> 36.5 us  [tensor_parallel(): lax.psum((downweight_grad, upweight_grad), 'rep')]
    psum x1, blocking collectives: 60.9 us -> 46.1 us  [tensor_parallel(): lax.psum(jnp.concatenate([vectors.reshape(-1), bias_slots.reshape(-1)]),...]
  transfers between devices with their start and end apart: 14 -> 7, of which waited for: 8 -> 3; matrix products, arithmetic and copies ran while one was open for 11% -> 12% of each run, Pallas kernels for 0% -> 38%
where the time goes in v2:
time: 506 us; the launch traced here: 500 us
  Pallas kernels  220 us (43%)
  waiting for transfers between devices  104 us (21%)
  local copies, waits for them, and re-layouts  47.4 us (9%)
  blocking collectives  46.1 us (9%)
  matrix products  33.2 us (7%)
  starting transfers between devices  19.3 us (4%)
  other arithmetic  15.5 us (3%)
  between operations  14.7 us (3%)
    pallas_call x3, Pallas kernels, gather_group(): pl.pallas_call(functools.partial(gather_kernel, shards, count), out_shape...  115 us
    pallas_call x4, Pallas kernels, scatter_group(): pl.pallas_call(functools.partial(scatter_kernel, shards), out_shape=jax.S...  105 us
    psum x1, waiting for transfers between devices, tensor_parallel(): lax.psum((projweight_grad, qkvweight_grad), 'rep')  50.4 us
    psum x1, blocking collectives, tensor_parallel(): lax.psum(jnp.concatenate([vectors.reshape(-1), bias_slots.reshape(-1)]),...  46.1 us
    psum x1, waiting for transfers between devices, tensor_parallel(): lax.psum((downweight_grad, upweight_grad), 'rep')  36.5 us
    unnamed x106, local copies, waits for them, and re-layouts  21.2 us
    all_to_all x2, waiting for transfers between devices, to_rows(): lax.all_to_all(split, GROUP, split_axis=0, concat_axis=2, tiled=True)  16.8 us
  transfers between devices with their start and end apart: 7, of which 3 were waited for; matrix products, arithmetic and copies ran while one was open for 12% of the time, Pallas kernels for 38%

profile of v2, /device:TPU:0, one launch (start us, length us, event | category | flops | bytes accessed | tf_op | source)
XLA Modules:
  0.0 500.3 jit_solution(18029155005596138660)
XLA Ops:
  8.0 1.5 copy.163
  10.6 6.5 %all-to-all-start = ((bf16[128,3,8,128]{0,3,1,2:T(8,128)(2,1)}), bf16[128,3,8,128]{0,3,1,2:T(8,128)(2,1)}, u32[]{:S(2)}, u32[]{:S(2)}) async-start(bf16[128,3,8,128]{0,3,1,2:T(8,128)(2,1)} %copy.164), calls=%async_computation | async-start | bytes 1572864 | tf_op jit(solution)/shard_map/all_to_all | solution.py:505
  19.0 59.7 %gather_group_0.1 = (bf16[8,128,1024]{2,1,0:T(8,128)(2,1)S(1)}, bf16[8,16,128]{2,1,0:T(8,128)(2,1)S(1)}) custom-call(bf16[128,1024]{1,0:T(8,128)(2,1)S(1)} %bitcast.231, bf16[16,128]{1,0:T(8,128)(2,1)S(1)} %pad_bitcast_fusion.refs_1_), custom_call_target="tpu_custom_call" | custom-call | tf_op jit(solution)/shard_map/gather_group_0/pallas_call | solution.py:347
  79.2 2.5 copy.175
  82.5 2.1 add_convert_fusion.1
  84.6 3.6 all-to-all-start.1
  88.2 1.6 copy.165
  89.9 3.1 fusion.24
  95.7 1.2 copy.171
  96.9 2.1 reshape.339
  99.0 1.2 copy.172
  103.4 28.9 %scatter_group_1.1 = f32[128,1024]{1,0:T(8,128)S(1)} custom-call(bf16[8,128,1024]{2,1,0:T(8,128)(2,1)S(1)} %bitcast.230), custom_call_target="tpu_custom_call" | custom-call | tf_op jit(solution)/shard_map/scatter_group_1/pallas_call | solution.py:417
  132.9 27.0 %gather_group_2.1 = bf16[8,128,1024]{2,1,0:T(8,128)(2,1)S(1)} custom-call(bf16[128,1024]{1,0:T(8,128)(2,1)S(1)} %add_convert_fusion.2.refs_0_), custom_call_target="tpu_custom_call" | custom-call | tf_op jit(solution)/shard_map/gather_group_2/pallas_call | solution.py:347
  159.9 1.3 copy-done.5
  161.2 1.3 copy.177
  162.5 4.5 multiply_convert_fusion.1
  167.1 1.3 convolution_convert_fusion.1
  168.3 27.2 %scatter_group_4.1 = f32[128,1024]{1,0:T(8,128)S(1)} custom-call(bf16[8,128,1024]{2,1,0:T(8,128)(2,1)S(1)} %bitcast.234), custom_call_target="tpu_custom_call" | custom-call | tf_op jit(solution)/shard_map/scatter_group_4/pallas_call | solution.py:417
  195.6 4.2 fusion.61
  199.8 2.3 fusion.15
  202.1 1.3 convolution_convert_fusion
  203.4 28.1 %scatter_group_3.1 = f32[128,1024]{1,0:T(8,128)S(1)} custom-call(bf16[8,128,1024]{2,1,0:T(8,128)(2,1)S(1)} %bitcast.233), custom_call_target="tpu_custom_call" | custom-call | tf_op jit(solution)/shard_map/scatter_group_3/pallas_call | solution.py:417
  231.5 2.3 fusion.12
  235.9 27.9 %gather_group_5.1 = bf16[8,128,1024]{2,1,0:T(8,128)(2,1)S(1)} custom-call(bf16[128,1024]{1,0:T(8,128)(2,1)S(1)} %multiply_convert_fusion.2.refs_0_), custom_call_target="tpu_custom_call" | custom-call | tf_op jit(solution)/shard_map/gather_group_5/pallas_call | solution.py:347
  263.9 1.4 convolution_convert_fusion.6
  265.3 2.0 reshape.342
  268.6 3.0 fusion.59
  272.6 36.5 %all-reduce.8.cloned.1.call-done = (bf16[1024,1,1,512]{3,0,2,1:T(8,128)(2,1)}, bf16[512,1024]{1,0:T(8,128)(2,1)}) async-done(((bf16[1024,1,1,512]{3,0,2,1:T(8,128)(2,1)}, bf16[512,1024]{1,0:T(8,128)(2,1)}), (bf16[1024,1,1,512]{3,0,2,1:T(8,128)(2,1)}, bf16[512,1024]{1,0:T(8,128)(2,1)})) %all-reduce.8.cloned.1.call-update) | async-done | bytes 2097168 | tf_op jit(solution)/shard_map/psum | solution.py:622
  309.6 3.3 reduce.6
  312.9 2.6 reshape.344
  315.5 4.6 all-to-all-start.2
  320.1 1.4 fusion.21
  325.6 2.2 fusion.56
  327.8 2.2 convolution_convert_fusion.4
  330.0 16.8 %all-to-all-done.2 = bf16[8,2,32768]{2,1,0:T(2,128)(2,1)} async-done(((bf16[8,2,32768]{2,1,0:T(2,128)(2,1)}), bf16[8,2,32768]{2,1,0:T(2,128)(2,1)}, u32[]{:S(2)}, u32[]{:S(2)}) %all-to-all-start.2) | async-done | bytes 1048608 | tf_op jit(solution)/shard_map/all_to_all | solution.py:510
  346.8 5.8 %reshape.345 = bf16[1024,1,1,512]{3,2,1,0:T(2,128)(2,1)} reshape(bf16[8,2,32768]{2,1,0:T(2,128)(2,1)} %all-to-all-done.2) | data formatting | bytes 2097152
  352.6 1.9 copy.208
  354.4 1.3 copy.191
  355.7 2.3 copy.192
  358.4 50.4 %all-reduce.6.cloned.1.call-done = (bf16[1024,3,1,128]{0,3,1,2:T(8,128)(2,1)}, bf16[128,1024]{1,0:T(8,128)(2,1)}) async-done(((bf16[1024,3,1,128]{0,3,1,2:T(8,128)(2,1)}, bf16[128,1024]{1,0:T(8,128)(2,1)}), (bf16[1024,3,1,128]{0,3,1,2:T(8,128)(2,1)}, bf16[128,1024]{1,0:T(8,128)(2,1)})) %all-reduce.6.cloned.1.call-update) | async-done | bytes 1048592 | tf_op jit(solution)/shard_map/psum | solution.py:627
  408.9 2.3 copy.193
  411.2 4.6 all-to-all-start.3
  415.9 46.1 %psum.35 = f32[14336]{0:T(1024)S(1)} all-reduce(f32[14336]{0:T(1024)S(1)} %pad_maximum_fusion), channel_id=1, replica_groups=mesh['rep'=4,'shard'=4,'seq'=2] {'rep','shard','seq'}, use_global_device_ids=true, to_apply=%region_24.25 | all-reduce | flops 14336 | bytes 114688 | tf_op jit(solution)/shard_map/psum | solution.py:613
  462.0 20.9 %scatter_group_6.1 = f32[128,1024]{1,0:T(8,128)S(1)} custom-call(bf16[8,128,1024]{2,1,0:T(8,128)(2,1)S(1)} %bitcast.232), custom_call_target="tpu_custom_call" | custom-call | tf_op jit(solution)/shard_map/scatter_group_6/pallas_call | solution.py:417
  486.1 1.6 copy.195
  487.7 1.6 convert_element_type.264
  490.1 1.4 convert_bitcast_fusion
  492.4 1.4 reshape.334
  (181 shorter events, 25.3 us)
Async XLA Ops:
  7.2 159.9 %copy-start = (bf16[512,1024]{1,0:T(8,128)(2,1)S(1)}, bf16[512,1024]{1,0:T(8,128)(2,1)}, u32[]{:S(2)}) copy-start(bf16[512,1024]{1,0:T(8,128)(2,1)} %param.33) | copy-start | bytes 3145732
  7.2 188.4 %all-gather.3.cloned.1.call-start = ((), (), s32[]{:S(2)}) async-start(), calls=%async_computation.4 | async-start | bytes 2359296 | tf_op jit(solution)/shard_map/all_gather | solution.py:273
  7.9 9.1 %copy-start.37 = (s32[1,256]{1,0:T(1,128)S(1)}, s32[1,256]{1,0:T(1,128)}, u32[]{:S(2)}) copy-start(s32[1,256]{1,0:T(1,128)} %param.19) | copy-start | bytes 3076
  8.0 9.1 %copy-start.4 = (bf16[1,128,1024]{2,1,0:T(8,128)(2,1)S(1)}, bf16[1,128,1024]{2,1,0:T(8,128)(2,1)}, u32[]{:S(2)}) copy-start(bf16[1,128,1024]{2,1,0:T(8,128)(2,1)} %param.18) | copy-start | bytes 786436
  9.5 7.7 %copy-start.28 = (bf16[128]{0:T(256)(128)(2,1)S(1)}, bf16[128]{0:T(256)(128)(2,1)}, u32[]{:S(2)}) copy-start(bf16[128]{0:T(256)(128)(2,1)} %param.21) | copy-start | bytes 772
  9.5 7.9 %copy-start.29 = (bf16[128]{0:T(256)(128)(2,1)S(1)}, bf16[128]{0:T(256)(128)(2,1)}, u32[]{:S(2)}) copy-start(bf16[128]{0:T(256)(128)(2,1)} %param.22) | copy-start | bytes 772
  9.5 8.1 %copy-start.30 = (bf16[128]{0:T(256)(128)(2,1)S(1)}, bf16[128]{0:T(256)(128)(2,1)}, u32[]{:S(2)}) copy-start(bf16[128]{0:T(256)(128)(2,1)} %param.27) | copy-start | bytes 772
  9.6 8.3 %copy-start.31 = (bf16[128]{0:T(256)(128)(2,1)S(1)}, bf16[128]{0:T(256)(128)(2,1)}, u32[]{:S(2)}) copy-start(bf16[128]{0:T(256)(128)(2,1)} %param.28) | copy-start | bytes 772
  9.6 8.5 %copy-start.32 = (bf16[128]{0:T(256)(128)(2,1)S(1)}, bf16[128]{0:T(256)(128)(2,1)}, u32[]{:S(2)}) copy-start(bf16[128]{0:T(256)(128)(2,1)} %param.29) | copy-start | bytes 772
  9.6 8.7 %copy-start.33 = (bf16[128]{0:T(256)(128)(2,1)S(1)}, bf16[128]{0:T(256)(128)(2,1)}, u32[]{:S(2)}) copy-start(bf16[128]{0:T(256)(128)(2,1)} %param.30) | copy-start | bytes 772
  9.6 8.9 %copy-start.34 = (bf16[128]{0:T(256)(128)(2,1)S(1)}, bf16[128]{0:T(256)(128)(2,1)}, u32[]{:S(2)}) copy-start(bf16[128]{0:T(256)(128)(2,1)} %param.34) | copy-start | bytes 772
  9.6 9.1 %copy-start.35 = (bf16[128]{0:T(256)(128)(2,1)S(1)}, bf16[128]{0:T(256)(128)(2,1)}, u32[]{:S(2)}) copy-start(bf16[128]{0:T(256)(128)(2,1)} %param.35) | copy-start | bytes 772
  10.5 68.6 %copy-start.38 = (bf16[128]{0:T(256)(128)(2,1)S(1)}, bf16[128]{0:T(256)(128)(2,1)}, u32[]{:S(2)}) copy-start(bf16[128]{0:T(256)(128)(2,1)} %param.24) | copy-start | bytes 772
  10.5 68.6 %copy-start.39 = (bf16[128]{0:T(256)(128)(2,1)S(1)}, bf16[128]{0:T(256)(128)(2,1)}, u32[]{:S(2)}) copy-start(bf16[128]{0:T(256)(128)(2,1)} %param.25) | copy-start | bytes 772
  10.5 68.6 %copy-start.27 = (bf16[512]{0:T(512)(128)(2,1)S(1)}, bf16[512]{0:T(512)(128)(2,1)}, u32[]{:S(2)}) copy-start(bf16[512]{0:T(512)(128)(2,1)} %param.32) | copy-start | bytes 3076
  10.6 74.1 %all-to-all-start = ((bf16[128,3,8,128]{0,3,1,2:T(8,128)(2,1)}), bf16[128,3,8,128]{0,3,1,2:T(8,128)(2,1)}, u32[]{:S(2)}, u32[]{:S(2)}) async-start(bf16[128,3,8,128]{0,3,1,2:T(8,128)(2,1)} %copy.164), calls=%async_computation | async-start | bytes 1572864 | tf_op jit(solution)/shard_map/all_to_all | solution.py:505
  78.7 3.7 copy-start.2
  84.6 76.6 %all-to-all-start.1 = ((bf16[128,1,8,512]{0,3,1,2:T(8,128)(2,1)}), bf16[128,1,8,512]{0,3,1,2:T(8,128)(2,1)S(1)}, u32[]{:S(2)}, u32[]{:S(2)}) async-start(bf16[128,1,8,512]{0,3,1,2:T(8,128)(2,1)} %bitcast.240), calls=%async_computation.1 | async-start | bytes 2097152 | tf_op jit(solution)/shard_map/all_to_all | solution.py:505
  88.2 220.9 %all-reduce.8.cloned.1.call-start = ((), (), s32[]{:S(2)}) async-start(), calls=%async_computation.6 | async-start | bytes 4194304 | tf_op jit(solution)/shard_map/psum | solution.py:622
  89.9 3.2 copy-start.24
  94.6 6.4 %copy-start.18 = (bf16[4,256,2,64]{1,3,2,0:T(8,128)(2,1)}, bf16[4,256,2,64]{1,3,2,0:T(8,128)(2,1)S(1)}, u32[]{:S(2)}) copy-start(bf16[4,256,2,64]{1,3,2,0:T(8,128)(2,1)S(1)} %copy.170) | copy-start | bytes 786436
  96.9 4.1 copy-start.16
  100.3 1.1 copy-start.12
  101.1 1.3 copy-start.7
  101.4 1.3 copy-start.20
  102.6 29.6 %copy-start.14 = (bf16[16,8,4,256]{3,1,2,0:T(8,128)(2,1)}, bf16[16,8,4,256]{3,1,2,0:T(8,128)(2,1)S(1)}, u32[]{:S(2)}) copy-start(bf16[16,8,4,256]{3,1,2,0:T(8,128)(2,1)S(1)} %copy.212) | copy-start | bytes 786436
  159.9 1.3 copy-start.5
  167.1 1.3 copy-start.40
  195.6 4.2 copy-start.6
  199.8 2.3 copy-start.23
  202.1 29.4 %copy-start.41 = (bf16[1024,512]{1,0:T(8,128)(2,1)S(1)}, bf16[1024,512]{1,0:T(8,128)(2,1)}, u32[]{:S(2)}) copy-start(bf16[1024,512]{1,0:T(8,128)(2,1)} %copy-done.40) | copy-start | bytes 3145732
  203.4 28.1 %copy-start.36 = (bf16[1,1024,1024]{2,1,0:T(8,128)(2,1)S(1)}, bf16[1,1024,1024]{2,1,0:T(8,128)(2,1)}, u32[]{:S(2)}) copy-start(bf16[1,1024,1024]{2,1,0:T(8,128)(2,1)} %all-gather.3.cloned.1.call-done) | copy-start | bytes 6291460
  235.9 29.4 %copy-start.9 = (f32[128,1024]{1,0:T(8,128)}, f32[128,1024]{1,0:T(8,128)S(1)}, u32[]{:S(2)}) copy-start(f32[128,1024]{1,0:T(8,128)S(1)} %get-tuple-element.72) | copy-start | bytes 1572868
  235.9 28.0 %copy-start.21 = (bf16[128,1024]{1,0:T(8,128)(2,1)S(1)}, bf16[128,1024]{1,0:T(8,128)(2,1)}, u32[]{:S(2)}) copy-start(bf16[128,1024]{1,0:T(8,128)(2,1)} %param.26) | copy-start | bytes 786436
  265.3 6.2 %copy-start.13 = (bf16[4,256,2,64]{1,3,2,0:T(8,128)(2,1)S(1)}, bf16[4,256,2,64]{1,3,2,0:T(8,128)(2,1)}, u32[]{:S(2)}) copy-start(bf16[4,256,2,64]{1,3,2,0:T(8,128)(2,1)} %copy-done.12) | copy-start | bytes 786436
  268.5 3.0 copy-start.8
  315.5 31.3 %all-to-all-start.2 = ((bf16[8,2,32768]{2,1,0:T(2,128)(2,1)}), bf16[8,2,32768]{2,1,0:T(2,128)(2,1)}, u32[]{:S(2)}, u32[]{:S(2)}) async-start(bf16[8,2,32768]{2,1,0:T(2,128)(2,1)} %reshape.344), calls=%async_computation.2 | async-start | bytes 2097152 | tf_op jit(solution)/shard_map/all_to_all | solution.py:510
  320.1 88.8 %all-reduce.6.cloned.1.call-start = ((), (), s32[]{:S(2)}) async-start(), calls=%async_computation.5 | async-start | bytes 2097152 | tf_op jit(solution)/shard_map/psum | solution.py:627
  320.1 2.9 copy-start.17
  323.0 1.0 copy-start.15
  323.7 1.6 copy-start.3
  323.7 1.9 copy-start.25
  411.2 78.9 %all-to-all-start.3 = ((bf16[1024,3,1,128]{3,1,2,0:T(4,128)(2,1)}), bf16[1024,3,1,128]{3,1,2,0:T(4,128)(2,1)}, u32[]{:S(2)}, u32[]{:S(2)}) async-start(bf16[1024,3,1,128]{3,1,2,0:T(4,128)(2,1)} %copy.193), calls=%async_computation.3 | async-start | bytes 2097152 | tf_op jit(solution)/shard_map/all_to_all | solution.py:510
  415.8 69.2 %copy-start.10 = (f32[128,1024]{1,0:T(8,128)S(1)}, f32[128,1024]{1,0:T(8,128)}, u32[]{:S(2)}) copy-start(f32[128,1024]{1,0:T(8,128)} %copy-done.9) | copy-start | bytes 1572868
  482.9 3.1 copy-start.11
  485.0 2.7 copy-start.19
  487.7 1.6 copy-start.26
  491.4 2.3 copy-start.1
  (1 other events, 0.9 us)
Sparse Core Ops, SparseCore 0:
  9.6 59.5 all-gather.2
  233.9 75.1 all-reduce.7
  358.2 50.6 all-reduce.5

commit v3 on v2

--- a/solution.py
+++ b/solution.py
@@ -433,7 +433,218 @@
     )(terms.reshape((2 * shards,) + block))
 
 
-def tensor_parallel(shards, seqs, *arguments):
+def exchange_kernel(shards, reps, with_scatter, *refs):
+    if with_scatter:
+        main, column, row, vectors, biases = refs[:5]
+        result, column_out, row_out, vectors_out = refs[5:9]
+        near, outgoing, arrived, column_near, column_sum, row_near, vector_in, vector_sum = refs[
+            9:17
+        ]
+        rest = refs[17:]
+        vector_near, rest = rest[0], rest[1:]
+    else:
+        main, column, row = refs[:3]
+        result, column_out, row_out = refs[3:6]
+        column_near, column_sum, row_near = refs[6:9]
+        rest = refs[9:]
+    send_sem, recv_sem, local_sem = rest
+    group = 2 * shards
+    rep = lax.axis_index("rep")
+    shard, seq = lax.axis_index("shard"), lax.axis_index("seq")
+    other = 1 - seq
+    place = 2 * shard + seq
+
+    def member(step):
+        at = lax.rem(place + step, group)
+        return at, {"shard": at // 2, "seq": lax.rem(at, 2)}
+
+    barrier = pltpu.get_barrier_semaphore()
+    for step in range(1, group):
+        pl.semaphore_signal(barrier, inc=1, device_id=member(step)[1])
+    for step in range(1, reps):
+        pl.semaphore_signal(barrier, inc=1, device_id={"rep": lax.rem(rep + step, reps)})
+    pl.semaphore_wait(barrier, group + reps - 2)
+
+    used = []
+
+    def push(source, target, device):
+        slot = len(used)
+        copy = pltpu.make_async_remote_copy(
+            src_ref=source,
+            dst_ref=target,
+            send_sem=send_sem.at[slot],
+            recv_sem=recv_sem.at[slot],
+            device_id=device,
+        )
+        copy.start()
+        used.append(copy)
+        return copy
+
+    def peer(step):
+        return lax.rem(rep + step, reps)
+
+    first, along, local = [], [], []
+    if with_scatter:
+        for step in range(1, shards + 1):
+            target = lax.rem(shard + step, shards)
+            first.append(push(main.at[2 * target + other], near.at[step - 1], {"seq": other}))
+    else:
+        for step in range(1, shards):
+            along.append(
+                push(main, result.at[place], {"shard": lax.rem(shard + step, shards)})
+            )
+        beside = push(main, result.at[place], {"seq": other})
+        copy = pltpu.make_async_copy(main, result.at[place], local_sem.at[0])
+        copy.start()
+        local.append(copy)
+    column_first = [
+        push(column.at[:, peer(step)], column_near.at[step - 1], {"rep": peer(step)})
+        for step in range(1, reps)
+    ]
+    row_first = [
+        push(row.at[peer(step)], row_near.at[step - 1], {"rep": peer(step)})
+        for step in range(1, reps)
+    ]
+    if with_scatter:
+        vector_first = []
+        for step in range(1, group):
+            at, device = member(step)
+            vector_first.append(push(vectors.at[at], vector_in.at[step - 1], device))
+
+    last = []
+    if with_scatter:
+        for step in range(1, shards + 1):
+            target = lax.rem(shard + step, shards)
+            first[step - 1].wait_recv()
+            both = main[2 * target + seq].astype(jnp.float32) + near[step - 1].astype(jnp.float32)
+            if step == shards:
+                result[...] = both
+            else:
+                outgoing[step - 1] = both.astype(jnp.bfloat16)
+                along.append(
+                    push(outgoing.at[step - 1], arrived.at[step - 1], {"shard": target})
+                )
+        half = vectors.shape[1]
+        total = vectors[place]
+        for step in range(1, group):
+            vector_first[step - 1].wait_recv()
+            total += vector_in[step - 1]
+        vector_sum[:half] = total
+        vector_sum[half:] = biases[...]
+        vector_second = [
+            push(vector_sum, vector_near.at[step - 1], {"rep": peer(step)})
+            for step in range(1, reps)
+        ]
+    else:
+        for step in range(1, shards):
+            along[step - 1].wait_recv()
+            origin = 2 * lax.rem(shard + shards - step, shards) + seq
+            last.append(push(result.at[origin], result.at[origin], {"seq": other}))
+        last.append(beside)
+
+    for copy in column_first:
+        copy.wait_recv()
+    total = column[:, rep].astype(jnp.float32)
+    for step in range(1, reps):
+        total += column_near[step - 1].astype(jnp.float32)
+    column_sum[...] = total.astype(jnp.bfloat16)
+    column_second = []
+    for step in range(1, group):
+        at, device = member(step)
+        column_second.append(push(column_sum.at[at], column_out.at[place, rep], device))
+    copy = pltpu.make_async_copy(column_sum.at[place], column_out.at[place, rep], local_sem.at[1])
+    copy.start()
+
+    for row_copy in row_first:
+        row_copy.wait_recv()
+    total = row[rep].astype(jnp.float32)
+    for step in range(1, reps):
+        total += row_near[step - 1].astype(jnp.float32)
+    row_out[rep] = total.astype(jnp.bfloat16)
+    for step in range(1, reps):
+        last.append(push(row_out.at[rep], row_out.at[rep], {"rep": peer(step)}))
+
+    copy.wait()
+    for column_copy in column_second:
+        column_copy.wait_recv()
+    for step in range(1, reps):
+        last.append(
+            push(column_out.at[:, rep], column_out.at[:, rep], {"rep": peer(step)})
+        )
+    if with_scatter:
+        for step in range(1, reps):
+            vector_second[step - 1].wait_recv()
+        total = vector_sum[...]
+        for step in range(1, reps):
+            total += vector_near[step - 1]
+        vectors_out[...] = total
+        for step in range(1, shards):
+            along[step - 1].wait_recv()
+            result[...] += arrived[step - 1].astype(jnp.float32)
+    for local_copy in local:
+        local_copy.wait()
+    for done in last:
+        done.wait_recv()
+    for done in used:
+        done.wait_send()
+
+
+def exchange(shards, reps, call, main, column, row, vectors=None, biases=None):
+    with_scatter = vectors is not None
+    group = 2 * shards
+    column = column.reshape(group, reps, column.shape[0] // (group * reps), -1)
+    row = row.reshape(reps, row.shape[0] // reps, -1)
+    part = (group,) + column.shape[2:]
+    low = jnp.bfloat16
+    scratch = [
+        pltpu.VMEM((reps - 1,) + part, low),
+        pltpu.VMEM(part, low),
+        pltpu.VMEM((reps - 1,) + row.shape[1:], low),
+    ]
+    outs = [jax.ShapeDtypeStruct(column.shape, low), jax.ShapeDtypeStruct(row.shape, low)]
+    operands = [column, row]
+    copies = 2 * (reps - 1) + (group - 1) + 2 * (reps - 1)
+    if with_scatter:
+        block = (main.shape[0] // group, main.shape[1])
+        main = main.astype(low).reshape((group,) + block)
+        summed = (vectors.shape[1] + biases.shape[0], vectors.shape[2])
+        scratch = [
+            pltpu.VMEM((shards,) + block, low),
+            pltpu.VMEM((shards - 1,) + block, low),
+            pltpu.VMEM((shards - 1,) + block, low),
+        ] + scratch
+        scratch += [
+            pltpu.VMEM((group - 1,) + vectors.shape[1:], jnp.float32),
+            pltpu.VMEM(summed, jnp.float32),
+            pltpu.VMEM((reps - 1,) + summed, jnp.float32),
+        ]
+        operands += [vectors, biases]
+        outs = [jax.ShapeDtypeStruct(block, jnp.float32)] + outs
+        outs += [jax.ShapeDtypeStruct(summed, jnp.float32)]
+        copies += (2 * shards - 1) + (group - 1) + (reps - 1)
+    else:
+        outs = [jax.ShapeDtypeStruct((group,) + main.shape, main.dtype)] + outs
+        copies += 2 * shards - 1
+    operands = [main] + operands
+    return pl.pallas_call(
+        functools.partial(exchange_kernel, shards, reps, with_scatter),
+        out_shape=outs,
+        in_specs=[pl.BlockSpec(memory_space=pltpu.VMEM)] * len(operands),
+        out_specs=[pl.BlockSpec(memory_space=pltpu.VMEM)] * len(outs),
+        scratch_shapes=scratch
+        + [
+            pltpu.SemaphoreType.DMA((copies,)),
+            pltpu.SemaphoreType.DMA((copies,)),
+            pltpu.SemaphoreType.DMA((2,)),
+        ],
+        compiler_params=pltpu.CompilerParams(
+            collective_id=call, has_side_effects=True, vmem_limit_bytes=VMEM_LIMIT
+        ),
+        name="exchange_%d" % call,
+    )(*operands)
+
+
+def tensor_parallel(reps, shards, seqs, *arguments):
     (
         tokens,
         key_valid,
@@ -505,10 +716,9 @@
         moved = lax.all_to_all(split, GROUP, split_axis=2, concat_axis=0, tiled=True)
         return moved.reshape(width, -1)
 
-    def to_rows(grad, parts):
-        split = grad.reshape(width, parts, 1, -1)
-        moved = lax.all_to_all(split, GROUP, split_axis=0, concat_axis=2, tiled=True)
-        return moved.reshape(own, -1)
+    def to_rows(moved, parts):
+        moved = moved.reshape(group, own, parts, -1).transpose(1, 2, 0, 3)
+        return moved.reshape(own, -1).astype(jnp.float32)
 
     qkv_own = to_columns(qkvweight, 3)
     up_own = to_columns(upweight, 1)
@@ -561,9 +771,17 @@
     out_grad = cotangent.reshape(rows, width).astype(jnp.float32)
     middle_grad = out_grad + norm_backward(acttwo_grad * gain_two, normed_two, spread_two)
     branchone_grad = middle_grad * scale_one
-    proj_low = gather_group(shards, 5, branchone_grad.astype(jnp.bfloat16))[0].reshape(
-        group * rows, width
-    )
+    proj_low, upweight_grad, downweight_grad = exchange(
+        shards,
+        reps,
+        5,
+        branchone_grad.astype(jnp.bfloat16),
+        upweight_grad,
+        downweight_grad,
+    )
+    proj_low = proj_low.reshape(group * rows, width)
+    upweight_grad = to_rows(upweight_grad, 1)
+    downweight_grad = downweight_grad.reshape(-1, width).astype(jnp.float32)
 
     block_out = middle + scale_two * branch_two
 
@@ -587,10 +805,7 @@
     )
     mixed_low = jnp.concatenate([query_grad, key_grad, value_grad], axis=1).astype(jnp.bfloat16)
     actone_part = times_transposed(mixed_low, qkv_own)
-    actone_grad = scatter_group(shards, 6, actone_part)
     qkvweight_grad = contract_rows(act_one, mixed_low).astype(jnp.bfloat16)
-    tokens_grad = middle_grad + norm_backward(actone_grad * gain_one, normed_one, spread_one)
-
     vectors = jnp.stack(
         [
             jnp.sum(actone_part * normed_one_all, axis=0),
@@ -603,46 +818,44 @@
             jnp.sum(out_grad * branch_two, axis=0),
         ]
     )
-    place = lax.axis_index(GROUP)
     biases = jnp.concatenate(
         [jnp.sum(query_grad, axis=0), jnp.sum(value_grad, axis=0), upbias_grad]
-    ).reshape(-1)
-    bias_slots = lax.dynamic_update_slice(
-        jnp.zeros((group, biases.shape[0]), jnp.float32), biases[None], (place, 0)
-    )
-    totals = lax.psum(
-        jnp.concatenate([vectors.reshape(-1), bias_slots.reshape(-1)]), ("rep",) + GROUP
-    )
-    vectors = totals[: 8 * width].reshape(8, width)
-    vectors = lax.dynamic_slice(vectors, (0, place * own), (8, own))
-    biases = lax.dynamic_slice(
-        totals[8 * width :].reshape(group, -1), (place, 0), (1, biases.shape[0])
-    )[0]
-
-    downweight_grad, upweight_grad = lax.psum((downweight_grad, upweight_grad), "rep")
-    upweight_grad = to_rows(upweight_grad, 1)
-    upweight_grad, downweight_grad, projweight_grad, qkvweight_grad = lax.optimization_barrier(
-        (upweight_grad, downweight_grad, projweight_grad, qkvweight_grad)
-    )
-    projweight_grad, qkvweight_grad = lax.psum((projweight_grad, qkvweight_grad), "rep")
+    )
+    used = biases.shape[0]
+    padded = -(-used // (8 * own)) * 8 * own
+    biases = jnp.pad(biases, (0, padded - used)).reshape(-1, own)
+    actone_grad, qkvweight_grad, projweight_grad, totals = exchange(
+        shards,
+        reps,
+        6,
+        actone_part,
+        qkvweight_grad,
+        projweight_grad,
+        vectors.reshape(8, group, own).transpose(1, 0, 2),
+        biases,
+    )
+    tokens_grad = middle_grad + norm_backward(actone_grad * gain_one, normed_one, spread_one)
+    vectors = totals[:8]
+    biases = totals[8:].reshape(-1)[:used]
     qkvweight_grad = to_rows(qkvweight_grad, 3)
+    projweight_grad = projweight_grad.reshape(own, width).astype(jnp.float32)
 
     return (
         block_out.reshape(images, tok_rows, width),
         tokens_grad.reshape(images, tok_rows, width),
         vectors[0],
         vectors[1],
-        qkvweight_grad.astype(jnp.float32),
+        qkvweight_grad,
         biases[:own],
         biases[own : 2 * own],
-        projweight_grad.astype(jnp.float32),
+        projweight_grad,
         vectors[2],
         vectors[3],
         vectors[4],
         vectors[5],
-        upweight_grad.astype(jnp.float32),
+        upweight_grad,
         biases[2 * own :],
-        downweight_grad.astype(jnp.float32),
+        downweight_grad,
         vectors[6],
         vectors[7],
     )
@@ -651,7 +864,7 @@
 def solution(mesh):
     shards, seqs = mesh.shape["shard"], mesh.shape["seq"]
     if seqs == 2 and HEADS % (shards * seqs) == 0:
-        body = functools.partial(tensor_parallel, shards, seqs)
+        body = functools.partial(tensor_parallel, mesh.shape["rep"], shards, seqs)
     else:
         body = per_device
     return jax.shard_map(

time: 506 us -> 385 us (0.76)
  waiting for transfers between devices: 104 us -> 0.69 us
  Pallas kernels: 220 us -> 270 us
  blocking collectives: 46.1 us -> 0 us
  starting transfers between devices: 19.3 us -> 10.9 us
    pallas_call x0 -> x2, Pallas kernels: none -> 103 us  [exchange(): pl.pallas_call(functools.partial(exchange_kernel, shards, reps, with_scat...]
    psum x2 -> x0, waiting for transfers between devices: 86.9 us -> none  [the longest x1 50.4 us: tensor_parallel(): lax.psum((projweight_grad, qkvweight_grad), 'rep')]
    psum x1 -> x0, blocking collectives: 46.1 us -> none  [tensor_parallel(): lax.psum(jnp.concatenate([vectors.reshape(-1), bias_slots.reshape(-1)]),...]
    pallas_call x3 -> x2, Pallas kernels: 115 us -> 87.8 us  [gather_group(): pl.pallas_call(functools.partial(gather_kernel, shards, count), out_shape...]
    pallas_call x4 -> x3, Pallas kernels: 105 us -> 79.4 us  [scatter_group(): pl.pallas_call(functools.partial(scatter_kernel, shards), out_shape=jax.S...]
    all_to_all x2 -> x0, waiting for transfers between devices: 16.8 us -> none  [to_rows(): lax.all_to_all(split, GROUP, split_axis=0, concat_axis=2, tiled=True)]
    all_to_all x2 -> x0, starting transfers between devices: 9.21 us -> none  [to_rows(): lax.all_to_all(split, GROUP, split_axis=0, concat_axis=2, tiled=True)]
    unnamed x106 -> x119, local copies, waits for them, and re-layouts: 21.2 us -> 18 us
  transfers between devices with their start and end apart: 7 -> 3, of which waited for: 3 -> 0; matrix products, arithmetic and copies ran while one was open for 12% -> 10% of each run, Pallas kernels for 38% -> 36%
where the time goes in v3:
time: 385 us; the launch traced here: 384 us
  Pallas kernels  270 us (70%)
  local copies, waits for them, and re-layouts  45.7 us (12%)
  matrix products  30.6 us (8%)
  between operations  14.9 us (4%)
  other arithmetic  11.3 us (3%)
  starting transfers between devices  10.9 us (3%)
    pallas_call x2, Pallas kernels, exchange(): pl.pallas_call(functools.partial(exchange_kernel, shards, reps, with_scat...  103 us
    pallas_call x2, Pallas kernels, gather_group(): pl.pallas_call(functools.partial(gather_kernel, shards, count), out_shape...  87.8 us
    pallas_call x3, Pallas kernels, scatter_group(): pl.pallas_call(functools.partial(scatter_kernel, shards), out_shape=jax.S...  79.4 us
    unnamed x119, local copies, waits for them, and re-layouts  18 us
    another operation x8, local copies, waits for them, and re-layouts, to_images(): matrix.transpose(0, 2, 1, 3, 4, 5)  13.9 us
    all_to_all x2, starting transfers between devices, to_columns(): lax.all_to_all(split, GROUP, split_axis=2, concat_axis=0, tiled=True)  10.9 us
    dot_general x4, matrix products, times_transposed(): lax.dot_general(left, weight, (((1,), (1,)), ((), ())), preferred_element...  9.61 us
  transfers between devices with their start and end apart: 3, of which 0 were waited for; matrix products, arithmetic and copies ran while one was open for 10% of the time, Pallas kernels for 36%

profile of v3, /device:TPU:0, one launch (start us, length us, event | category | flops | bytes accessed | tf_op | source)
XLA Modules:
  0.0 384.2 jit_solution(12251775595631883247)
XLA Ops:
  8.0 1.5 copy.128
  9.6 1.0 copy.129
  10.6 6.5 %all-to-all-start = ((bf16[128,3,8,128]{0,3,1,2:T(8,128)(2,1)}), bf16[128,3,8,128]{0,3,1,2:T(8,128)(2,1)}, u32[]{:S(2)}, u32[]{:S(2)}) async-start(bf16[128,3,8,128]{0,3,1,2:T(8,128)(2,1)} %copy.129), calls=%async_computation | async-start | bytes 1572864 | tf_op jit(solution)/shard_map/all_to_all | solution.py:716
  19.0 59.7 %gather_group_0.1 = (bf16[8,128,1024]{2,1,0:T(8,128)(2,1)S(1)}, bf16[8,16,128]{2,1,0:T(8,128)(2,1)S(1)}) custom-call(bf16[128,1024]{1,0:T(8,128)(2,1)S(1)} %bitcast.240, bf16[16,128]{1,0:T(8,128)(2,1)S(1)} %pad_bitcast_fusion.refs_1_), custom_call_target="tpu_custom_call" | custom-call | tf_op jit(solution)/shard_map/gather_group_0/pallas_call | solution.py:347
  79.2 2.3 copy.140
  82.2 2.1 add_convert_fusion.1
  84.4 4.4 %all-to-all-start.1 = ((bf16[128,1,8,512]{0,3,1,2:T(8,128)(2,1)}), bf16[128,1,8,512]{0,3,1,2:T(8,128)(2,1)}, u32[]{:S(2)}, u32[]{:S(2)}) async-start(bf16[128,1,8,512]{0,3,1,2:T(8,128)(2,1)} %bitcast.255), calls=%async_computation.1 | async-start | bytes 2097152 | tf_op jit(solution)/shard_map/all_to_all | solution.py:716
  88.8 1.6 copy.130
  90.4 3.1 fusion.23
  95.2 2.0 reshape.361
  97.2 1.9 copy.135
  99.1 2.0 reshape.362
  101.1 1.9 copy.136
  102.9 2.0 reshape.360
  104.9 1.9 copy.137
  106.8 1.6 fusion.60
  110.7 23.7 %scatter_group_1.1 = f32[128,1024]{1,0:T(8,128)S(1)} custom-call(bf16[8,128,1024]{2,1,0:T(8,128)(2,1)S(1)} %bitcast.239), custom_call_target="tpu_custom_call" | custom-call | tf_op jit(solution)/shard_map/scatter_group_1/pallas_call | solution.py:417
  136.4 28.1 %gather_group_2.1 = bf16[8,128,1024]{2,1,0:T(8,128)(2,1)S(1)} custom-call(bf16[128,1024]{1,0:T(8,128)(2,1)S(1)} %add_convert_fusion.2.refs_0_), custom_call_target="tpu_custom_call" | custom-call | tf_op jit(solution)/shard_map/gather_group_2/pallas_call | solution.py:347
  164.5 1.3 copy-done.6
  165.8 2.3 copy.142
  168.1 4.5 %multiply_convert_fusion.1 = (bf16[1024,512]{1,0:T(8,128)(2,1)S(1)}, f32[1024,512]{1,0:T(8,128)}) fusion(f32[512]{0:T(512)S(1)} %convert_element_type.254, bf16[1024,1024]{1,0:T(8,128)(2,1)} %bitcast.244, bf16[1024,512]{1,0:T(8,128)(2,1)} %bitcast.261), kind=kOutput, calls=%fused_computation.18 | convolution fusion | flops 1076887552 | bytes 6293504 | tf_op jit(solution)/shard_map/dot_general | solution.py:756
  172.6 1.3 convolution_convert_fusion.1
  173.9 27.7 %scatter_group_4.1 = f32[128,1024]{1,0:T(8,128)S(1)} custom-call(bf16[8,128,1024]{2,1,0:T(8,128)(2,1)S(1)} %bitcast.242), custom_call_target="tpu_custom_call" | custom-call | tf_op jit(solution)/shard_map/scatter_group_4/pallas_call | solution.py:417
  202.4 4.4 %fusion.61 = (f32[512]{0:T(512)S(1)}, bf16[1024,512]{1,0:T(8,128)(2,1)S(1)}) fusion(f32[1024,512]{1,0:T(8,128)} %get-tuple-element.139, f32[512]{0:T(512)S(1)} %convert_element_type.254, bf16[512,1024]{1,0:T(8,128)(2,1)S(1)} %copy-done, bf16[1,1024,1024]{2,1,0:T(8,128)(2,1)} %all-gather.3.cloned.1.call-done, f32[1024]{0:T(1024)S(1)} %get-tuple-element.114), kind=kOutput, calls=%fused_computation.143 | convolution fusion | flops 1083178496 | bytes 6299648 | tf_op jit(solution)/shard_map/dot_general | solution.py:58
  206.8 1.3 convolution_convert_fusion.3
  208.1 1.3 convolution_convert_fusion
  209.4 28.1 %scatter_group_3.1 = f32[128,1024]{1,0:T(8,128)S(1)} custom-call(bf16[8,128,1024]{2,1,0:T(8,128)(2,1)S(1)} %bitcast.241), custom_call_target="tpu_custom_call" | custom-call | tf_op jit(solution)/shard_map/scatter_group_3/pallas_call | solution.py:417
  237.8 1.2 fusion.38
  239.9 1.3 fusion.12
  241.2 58.0 %exchange_5.1 = (bf16[8,128,1024]{2,1,0:T(8,128)(2,1)S(1)}, bf16[8,4,32,512]{3,2,1,0:T(8,128)(2,1)S(1)}, bf16[4,128,1024]{2,1,0:T(8,128)(2,1)S(1)}) custom-call(bf16[128,1024]{1,0:T(8,128)(2,1)S(1)} %multiply_convert_fusion.2.refs_0_, bf16[8,4,32,512]{3,2,1,0:T(8,128)(2,1)S(1)} %bitcast.247, bf16[4,128,1024]{2,1,0:T(8,128)(2,1)S(1)} %bitcast.248), custom_call_target="tpu_custom_call" | custom-call | tf_op jit(solution)/shard_map/exchange_5/pallas_call | solution.py:629
  299.2 1.0 copy-done.12
  300.2 1.0 copy-done.14
  302.3 1.1 reshape.363
  303.4 1.2 copy.144
  304.6 2.3 fusion.59
  308.5 1.1 fusion.20
  309.6 1.0 fusion.58
  311.1 1.2 copy.151
  312.3 1.2 copy.148
  313.6 3.2 fusion.56
  316.8 1.3 convolution_convert_fusion.4
  318.4 44.9 %exchange_6.1 = (f32[128,1024]{1,0:T(8,128)S(1)}, bf16[8,4,32,384]{3,2,1,0:T(8,128)(2,1)S(1)}, bf16[4,32,1024]{2,1,0:T(8,128)(2,1)S(1)}, f32[16,128]{1,0:T(8,128)S(1)}) custom-call(bf16[8,128,1024]{2,1,0:T(8,128)(2,1)S(1)} %bitcast.243, bf16[8,4,32,384]{3,2,1,0:T(8,128)(2,1)S(1)} %bitcast.249, bf16[4,32,1024]{2,1,0:T(8,128)(2,1)S(1)} %bitcast.246, ...), custom_call_target="tpu_custom_call" | custom-call | tf_op jit(solution)/shard_map/exchange_6/pallas_call | solution.py:629
  365.7 2.4 reshape.355
  368.1 1.6 copy.155
  369.7 3.1 copy.157
  373.1 1.6 copy.177
  374.7 1.6 bitcast_convert_fusion
  376.4 1.0 fusion.35
  (167 shorter events, 17.8 us)
Async XLA Ops:
  7.2 165.4 %copy-start = (bf16[512,1024]{1,0:T(8,128)(2,1)S(1)}, bf16[512,1024]{1,0:T(8,128)(2,1)}, u32[]{:S(2)}) copy-start(bf16[512,1024]{1,0:T(8,128)(2,1)} %param.33) | copy-start | bytes 3145732
  7.2 195.1 %all-gather.3.cloned.1.call-start = ((), (), s32[]{:S(2)}) async-start(), calls=%async_computation.2 | async-start | bytes 2359296 | tf_op jit(solution)/shard_map/all_gather | solution.py:273
  7.9 9.1 %copy-start.45 = (s32[1,256]{1,0:T(1,128)S(1)}, s32[1,256]{1,0:T(1,128)}, u32[]{:S(2)}) copy-start(s32[1,256]{1,0:T(1,128)} %param.19) | copy-start | bytes 3076
  8.0 9.1 %copy-start.2 = (bf16[1,128,1024]{2,1,0:T(8,128)(2,1)S(1)}, bf16[1,128,1024]{2,1,0:T(8,128)(2,1)}, u32[]{:S(2)}) copy-start(bf16[1,128,1024]{2,1,0:T(8,128)(2,1)} %param.18) | copy-start | bytes 786436
  9.5 7.7 %copy-start.36 = (bf16[128]{0:T(256)(128)(2,1)S(1)}, bf16[128]{0:T(256)(128)(2,1)}, u32[]{:S(2)}) copy-start(bf16[128]{0:T(256)(128)(2,1)} %param.21) | copy-start | bytes 772
  9.5 7.9 %copy-start.37 = (bf16[128]{0:T(256)(128)(2,1)S(1)}, bf16[128]{0:T(256)(128)(2,1)}, u32[]{:S(2)}) copy-start(bf16[128]{0:T(256)(128)(2,1)} %param.22) | copy-start | bytes 772
  9.5 8.1 %copy-start.38 = (bf16[128]{0:T(256)(128)(2,1)S(1)}, bf16[128]{0:T(256)(128)(2,1)}, u32[]{:S(2)}) copy-start(bf16[128]{0:T(256)(128)(2,1)} %param.27) | copy-start | bytes 772
  9.6 8.3 %copy-start.39 = (bf16[128]{0:T(256)(128)(2,1)S(1)}, bf16[128]{0:T(256)(128)(2,1)}, u32[]{:S(2)}) copy-start(bf16[128]{0:T(256)(128)(2,1)} %param.28) | copy-start | bytes 772
  9.6 8.5 %copy-start.40 = (bf16[128]{0:T(256)(128)(2,1)S(1)}, bf16[128]{0:T(256)(128)(2,1)}, u32[]{:S(2)}) copy-start(bf16[128]{0:T(256)(128)(2,1)} %param.29) | copy-start | bytes 772
  9.6 8.8 %copy-start.41 = (bf16[128]{0:T(256)(128)(2,1)S(1)}, bf16[128]{0:T(256)(128)(2,1)}, u32[]{:S(2)}) copy-start(bf16[128]{0:T(256)(128)(2,1)} %param.30) | copy-start | bytes 772
  9.6 9.0 %copy-start.42 = (bf16[128]{0:T(256)(128)(2,1)S(1)}, bf16[128]{0:T(256)(128)(2,1)}, u32[]{:S(2)}) copy-start(bf16[128]{0:T(256)(128)(2,1)} %param.34) | copy-start | bytes 772
  9.6 9.2 %copy-start.43 = (bf16[128]{0:T(256)(128)(2,1)S(1)}, bf16[128]{0:T(256)(128)(2,1)}, u32[]{:S(2)}) copy-start(bf16[128]{0:T(256)(128)(2,1)} %param.35) | copy-start | bytes 772
  10.6 68.6 %copy-start.46 = (bf16[128]{0:T(256)(128)(2,1)S(1)}, bf16[128]{0:T(256)(128)(2,1)}, u32[]{:S(2)}) copy-start(bf16[128]{0:T(256)(128)(2,1)} %param.24) | copy-start | bytes 772
  10.6 68.6 %copy-start.47 = (bf16[128]{0:T(256)(128)(2,1)S(1)}, bf16[128]{0:T(256)(128)(2,1)}, u32[]{:S(2)}) copy-start(bf16[128]{0:T(256)(128)(2,1)} %param.25) | copy-start | bytes 772
  10.6 68.6 %copy-start.35 = (bf16[512]{0:T(512)(128)(2,1)S(1)}, bf16[512]{0:T(512)(128)(2,1)}, u32[]{:S(2)}) copy-start(bf16[512]{0:T(512)(128)(2,1)} %param.32) | copy-start | bytes 3076
  10.6 73.8 %all-to-all-start = ((bf16[128,3,8,128]{0,3,1,2:T(8,128)(2,1)}), bf16[128,3,8,128]{0,3,1,2:T(8,128)(2,1)}, u32[]{:S(2)}, u32[]{:S(2)}) async-start(bf16[128,3,8,128]{0,3,1,2:T(8,128)(2,1)} %copy.129), calls=%async_computation | async-start | bytes 1572864 | tf_op jit(solution)/shard_map/all_to_all | solution.py:716
  84.4 81.4 %all-to-all-start.1 = ((bf16[128,1,8,512]{0,3,1,2:T(8,128)(2,1)}), bf16[128,1,8,512]{0,3,1,2:T(8,128)(2,1)}, u32[]{:S(2)}, u32[]{:S(2)}) async-start(bf16[128,1,8,512]{0,3,1,2:T(8,128)(2,1)} %bitcast.255), calls=%async_computation.1 | async-start | bytes 2097152 | tf_op jit(solution)/shard_map/all_to_all | solution.py:716
  90.4 3.2 copy-start.33
  106.8 1.9 copy-start.23
  108.4 1.3 copy-start.17
  108.7 1.3 copy-start.29
  164.5 1.3 copy-start.6
  172.6 1.3 copy-start.48
  202.4 4.4 %copy-start.7 = (bf16[8,128,1024]{2,1,0:T(8,128)(2,1)S(1)}, bf16[8,128,1024]{2,1,0:T(8,128)(2,1)}, u32[]{:S(2)}) copy-start(bf16[8,128,1024]{2,1,0:T(8,128)(2,1)} %copy-done.6) | copy-start | bytes 6291460
  206.8 1.3 copy-start.32
  209.4 28.1 %copy-start.20 = (f32[128,1024]{1,0:T(8,128)S(1)}, f32[128,1024]{1,0:T(8,128)}, u32[]{:S(2)}) copy-start(f32[128,1024]{1,0:T(8,128)} %copy-done.19) | copy-start | bytes 1572868
  209.4 28.4 %copy-start.4 = (f32[128,1024]{1,0:T(8,128)S(1)}, f32[128,1024]{1,0:T(8,128)}, u32[]{:S(2)}) copy-start(f32[128,1024]{1,0:T(8,128)} %copy-done.3) | copy-start | bytes 1572868
  209.4 28.4 %copy-start.9 = (f32[128,1024]{1,0:T(8,128)S(1)}, f32[128,1024]{1,0:T(8,128)}, u32[]{:S(2)}) copy-start(f32[128,1024]{1,0:T(8,128)} %copy-done.8) | copy-start | bytes 1572868
  209.4 28.4 %copy-start.31 = (bf16[1,128,1024]{2,1,0:T(8,128)(2,1)S(1)}, bf16[1,128,1024]{2,1,0:T(8,128)(2,1)}, u32[]{:S(2)}) copy-start(bf16[1,128,1024]{2,1,0:T(8,128)(2,1)} %param.20) | copy-start | bytes 786436
  237.8 2.1 copy-start.44
  237.8 2.1 copy-start.49
  241.2 59.9 %copy-start.26 = (bf16[16,8,4,256]{3,1,2,0:T(8,128)(2,1)S(1)}, bf16[16,8,4,256]{3,1,2,0:T(8,128)(2,1)}, u32[]{:S(2)}) copy-start(bf16[16,8,4,256]{3,1,2,0:T(8,128)(2,1)} %copy-done.25) | copy-start | bytes 786436
  241.2 60.4 %copy-start.30 = (bf16[128,1024]{1,0:T(8,128)(2,1)S(1)}, bf16[128,1024]{1,0:T(8,128)(2,1)}, u32[]{:S(2)}) copy-start(bf16[128,1024]{1,0:T(8,128)(2,1)} %param.26) | copy-start | bytes 786436
  299.2 1.0 copy-start.12
  300.2 1.0 copy-start.14
  302.3 4.6 %copy-start.24 = (bf16[4,256,2,64]{1,3,2,0:T(8,128)(2,1)S(1)}, bf16[4,256,2,64]{1,3,2,0:T(8,128)(2,1)}, u32[]{:S(2)}) copy-start(bf16[4,256,2,64]{1,3,2,0:T(8,128)(2,1)} %copy.137) | copy-start | bytes 786436
  304.6 2.3 copy-start.18
  307.5 1.0 copy-start.27
  307.5 2.1 copy-start.28
  311.0 2.6 copy-start.34
  316.8 1.6 copy-start.5
  363.3 1.2 copy-start.10
  363.4 1.4 copy-start.16
  369.7 3.1 copy-start.15
  373.1 1.6 copy-start.13
  374.7 1.6 copy-start.11
  374.7 1.6 copy-start.22
  374.7 2.7 copy-start.1
  (5 other events, 3.9 us)
Sparse Core Ops, SparseCore 0:
  9.6 59.5 all-gather.2
